TPU v7x, 32 devices: a whole 2x2x4 slice. The times are simulated.
32 devices in a mesh: ctx: 16 (over z, y, core), head: 2 (over x).
Axes of the slice: x: 2, y: 2, z: 4, core: 2. Of those that a mesh axis runs over, the one named last changes fastest.
Arguments:
- features: bfloat16 [8192, 5376], P('ctx', 'head'), may hold values from -30 to 30
- query_weight: bfloat16 [5376, 4096], P('ctx', 'head'), as said below
- key_weight: bfloat16 [5376, 2048], P('ctx', 'head'), as said below
- value_weight: bfloat16 [5376, 2048], P('ctx', 'head'), may hold values from -0.078125 to 0.078125
- doc_lengths: int32 [4], replicated, may hold values from 1 to 4096, 8192 in all
- out_grad: bfloat16 [8192, 4096], P('ctx', 'head'), may hold values from -6 to 6
Outputs:
- attention: bfloat16 [8192, 4096], P('ctx', 'head')
- key_weight_grad: bfloat16 [5376, 2048], P('ctx', 'head')
- value_weight_grad: bfloat16 [5376, 2048], P('ctx', 'head')
Inputs may be any that keep to these rules, and one draw needn't show every extreme that they name: `doc_lengths`: the lengths sum to 8192; the longest document holds half of them. `query_weight`: projection entries. `key_weight`: projection entries.
All inputs are finite; a program needn't handle non-finite values.
Results may differ from a plain program's by a relative error of at most 0.029.
Values may be sent and summed in bfloat16 or wider, within the bound.
A program may use at most 192 MiB of HBM per device.

v0:
```python
import jax
import jax.numpy as jnp
from jax import lax
from jax.sharding import PartitionSpec as P

D = 5376
HEADS_Q = 32
HEAD_DIM = 128
WINDOW = 1024
SPAN = 2


ROPE_BASE = 10000.0


def passed_along(block, axis, distance):
    devices = range(lax.axis_size(axis))
    route = [(i - distance, i) for i in devices if i - distance in devices]
    return lax.ppermute(block, axis, route)


def rotate_half(values):
    middle = values.shape[-1] // 2
    return jnp.concatenate([-values[..., middle:], values[..., :middle]], axis=-1)


def rope_tables(offsets):
    middle = HEAD_DIM // 2
    inverse = ROPE_BASE ** (-(jnp.arange(middle).astype(jnp.float32) * 2.0 / HEAD_DIM))
    angles = offsets.astype(jnp.float32)[:, None] * inverse[None, :]
    cosine = jnp.cos(angles)
    sine_table = jnp.sin(angles)
    return (
        jnp.concatenate([cosine, cosine], axis=-1),
        jnp.concatenate([sine_table, sine_table], axis=-1),
    )


def rotate(values, cosine, sine_table):
    return values * cosine[:, None, :] + rotate_half(values) * sine_table[:, None, :]


def unrotate(values, cosine, sine_table):
    return values * cosine[:, None, :] - rotate_half(values) * sine_table[:, None, :]


def start_of(positions, starts):
    candidates = jnp.where(starts[None, :] <= positions[:, None], starts[None, :], -1)
    return jnp.max(candidates, axis=1)


def shards(features, query_weight, key_weight, value_weight, doc_lengths, out_grad):
    tok_rows = features.shape[0]
    query_cols = query_weight.shape[1]
    value_cols = key_weight.shape[1]
    query_heads = query_cols // HEAD_DIM
    value_heads = value_cols // HEAD_DIM
    group_size = query_heads // value_heads
    query_scale = (D / HEADS_Q) ** (-0.5)
    ctx_index = lax.axis_index("ctx")
    gathered = lax.all_gather(features, "head", axis=1, tiled=True)

    def add_product(weight_piece):
        return jnp.dot(gathered, weight_piece, preferred_element_type=jnp.float32)

    pieces = (
        lax.all_gather(query_weight, "ctx", axis=0, tiled=True),
        lax.all_gather(key_weight, "ctx", axis=0, tiled=True),
        lax.all_gather(value_weight, "ctx", axis=0, tiled=True),
    )
    query_proj, key_proj, value_proj = tuple((add_product(weight_piece) for weight_piece in pieces))
    starts = jnp.cumsum(doc_lengths) - doc_lengths
    query_index = ctx_index * tok_rows + jnp.arange(tok_rows, dtype=jnp.int32)
    query_start = start_of(query_index, starts)
    cosine, sine_table = rope_tables(query_index - query_start)
    queries = (
        rotate(query_proj.reshape(tok_rows, query_heads, HEAD_DIM), cosine, sine_table)
        * query_scale
    ).astype(jnp.bfloat16)
    own_keys = rotate(key_proj.reshape(tok_rows, value_heads, HEAD_DIM), cosine, sine_table).astype(
        jnp.bfloat16
    )
    own_values = value_proj.reshape(tok_rows, value_heads, HEAD_DIM).astype(jnp.bfloat16)
    key_value = jnp.stack([own_keys, own_values])
    earlier = []
    moving = key_value
    for distance in range(1, SPAN + 1):
        moving = passed_along(moving, "ctx", 1)
        earlier.insert(0, moving)
    key_block = jnp.concatenate(earlier + [key_value], axis=1)
    key_rows = key_block.shape[1]
    key_index = (ctx_index - SPAN) * tok_rows + jnp.arange(key_rows, dtype=jnp.int32)
    key_start = start_of(key_index, starts)
    offsets_qk = query_index[:, None] - key_index[None, :]
    allowed = (
        (key_index[None, :] >= 0)
        & (offsets_qk >= 0)
        & (offsets_qk < WINDOW)
        & (query_start[:, None] == key_start[None, :])
    )
    grouped = queries.reshape(tok_rows, value_heads, group_size, HEAD_DIM)
    scores = jnp.einsum("tkgd,skd->kgts", grouped, key_block[0], preferred_element_type=jnp.float32)
    row_max = jnp.max(jnp.where(allowed, scores, -jnp.inf), axis=-1, keepdims=True)
    raw_weights = jnp.where(allowed, jnp.exp(scores - row_max), 0.0)
    prob_soft = raw_weights / jnp.sum(raw_weights, axis=-1, keepdims=True)
    probs_low = prob_soft.astype(jnp.bfloat16)
    attended = jnp.einsum(
        "kgts,skd->tkgd", probs_low, key_block[1], preferred_element_type=jnp.float32
    ).astype(jnp.bfloat16)
    attention = attended.reshape(tok_rows, query_cols)
    grad_heads = out_grad.reshape(tok_rows, value_heads, group_size, HEAD_DIM)
    out_dot = jnp.sum(
        grad_heads.astype(jnp.float32) * attended.astype(jnp.float32), axis=-1
    ).transpose(1, 2, 0)[..., None]
    value_partial = jnp.einsum(
        "kgts,tkgd->skd", probs_low, grad_heads, preferred_element_type=jnp.float32
    )
    prob_grad = jnp.einsum(
        "tkgd,skd->kgts", grad_heads, key_block[1], preferred_element_type=jnp.float32
    )
    score_grad = (prob_soft * (prob_grad - out_dot)).astype(jnp.bfloat16)
    key_partial = jnp.einsum(
        "kgts,tkgd->skd", score_grad, grouped, preferred_element_type=jnp.float32
    )
    partials = jnp.stack([key_partial, value_partial])

    def piece_of(distance):
        return partials[:, (SPAN - distance) * tok_rows : (SPAN - distance + 1) * tok_rows]

    returned = piece_of(SPAN)
    for distance in range(SPAN, 0, -1):
        returned = passed_along(returned.astype(jnp.bfloat16), "ctx", -1).astype(
            returned.dtype
        ) + piece_of(distance - 1)
    key_grad = (
        unrotate(returned[0], cosine, sine_table).astype(jnp.bfloat16).reshape(tok_rows, value_cols)
    )
    value_grad = returned[1].astype(jnp.bfloat16).reshape(tok_rows, value_cols)
    pair_grads = jnp.concatenate([key_grad, value_grad], axis=1)
    weight_grads = lax.psum_scatter(
        lax.dot_general(
            gathered, pair_grads, (((0,), (0,)), ((), ())), preferred_element_type=jnp.float32
        ).astype(jnp.bfloat16),
        "ctx",
        scatter_dimension=0,
        tiled=True,
    ).astype(jnp.float32)
    return (
        attention,
        weight_grads[:, :value_cols].astype(jnp.bfloat16),
        weight_grads[:, value_cols:].astype(jnp.bfloat16),
    )


def solution(mesh):
    placed = (
        P("ctx", "head"),
        P("ctx", "head"),
        P("ctx", "head"),
        P("ctx", "head"),
        P(),
        P("ctx", "head"),
    )
    return jax.shard_map(
        shards,
        mesh=mesh,
        in_specs=placed,
        out_specs=(P("ctx", "head"), P("ctx", "head"), P("ctx", "head")),
        check_vma=False,
    )
```

profile of v0, /device:TPU:0, one launch (start us, length us, event | category | flops | bytes accessed | tf_op | source)
XLA Modules:
  0.0 895.4 jit_solution(9235464230529267570)
XLA Ops:
  10.3 1.0 multiply_cosine_fusion
  12.2 71.6 %all-gather.5.cloned.1.call-done = bf16[512,5376]{1,0:T(8,128)(2,1)} async-done(((bf16[512,2688]{1,0:T(8,128)(2,1)}), bf16[512,5376]{1,0:T(8,128)(2,1)}) %all-gather.5.cloned.1.call-update) | async-done | bytes 5505040 | tf_op jit(solution)/shard_map/all_gather | solution.py:61
  83.8 93.4 %all-gather.7.cloned.1.call-done = bf16[5376,1024]{1,0:T(8,128)(2,1)} async-done(((bf16[336,1024]{1,0:T(8,128)(2,1)}), bf16[5376,1024]{1,0:T(8,128)(2,1)}) %all-gather.7.cloned.1.call-update) | async-done | bytes 11010064 | tf_op jit(solution)/shard_map/all_gather | solution.py:68
  177.3 10.2 %convolution_bitcast_fusion.1 = f32[64,8,8,128]{3,1,2,0:T(8,128)S(1)} fusion(bf16[512,5376]{1,0:T(8,128)(2,1)} %all-gather.5.cloned.1.call-done, bf16[5376,1024]{1,0:T(8,128)(2,1)} %all-gather.7.cloned.1.call-done), kind=kOutput, calls=%fused_computation.63 | convolution fusion | flops 5637144576 | bytes 18612224 | tf_op jit(solution)/shard_map/dot_general | solution.py:64
  188.0 80.9 %all-gather.9.cloned.1.call-done = bf16[5376,1024]{1,0:T(8,128)(2,1)} async-done(((bf16[336,1024]{1,0:T(8,128)(2,1)}), bf16[5376,1024]{1,0:T(8,128)(2,1)}) %all-gather.9.cloned.1.call-update) | async-done | bytes 11010064 | tf_op jit(solution)/shard_map/all_gather | solution.py:69
  268.9 10.2 %fusion.36 = bf16[64,8,8,128]{3,1,2,0:T(8,128)(2,1)S(1)} fusion(bf16[512,5376]{1,0:T(8,128)(2,1)} %all-gather.5.cloned.1.call-done, bf16[5376,1024]{1,0:T(8,128)(2,1)} %all-gather.9.cloned.1.call-done), kind=kOutput, calls=%fused_computation.65 | convolution fusion | flops 5637668864 | bytes 17563648 | tf_op jit(solution)/shard_map/dot_general | solution.py:64
  282.2 3.5 collective-permute-start
  285.7 2.6 collective-permute-done
  288.3 67.6 %collective-permute-start.1 = (bf16[2,512,8,128]{3,1,2,0:T(8,128)(2,1)}, bf16[2,512,8,128]{3,1,2,0:T(8,128)(2,1)}, u32[]{:S(2)}, u32[]{:S(2)}) collective-permute-start(bf16[2,512,8,128]{3,1,2,0:T(8,128)(2,1)} %collective-permute-done), channel_id=1, source_target_pairs={{0,2},{2,4},{4,6},{6,8},{8,10},{10,12},{12,14},{14,16},{16,18},{18... | collective-permute-start | bytes 6291464 | tf_op jit(solution)/shard_map/ppermute | solution.py:19
  356.9 2.9 copy.81
  359.9 2.7 fusion.25
  362.6 5.9 maximum_maximum_fusion
  368.5 53.7 %all-gather.11.cloned.1.call-done = bf16[5376,2048]{1,0:T(8,128)(2,1)} async-done(((bf16[336,2048]{1,0:T(8,128)(2,1)}), bf16[5376,2048]{1,0:T(8,128)(2,1)}) %all-gather.11.cloned.1.call-update) | async-done | bytes 22020112 | tf_op jit(solution)/shard_map/all_gather | solution.py:67
  422.2 16.5 %fusion.43 = f32[512,2048]{0,1:T(8,128)S(1)} fusion(bf16[512,5376]{1,0:T(8,128)(2,1)} %all-gather.5.cloned.1.call-done, bf16[5376,2048]{1,0:T(8,128)(2,1)} %all-gather.11.cloned.1.call-done), kind=kOutput, calls=%fused_computation.86 | convolution fusion | flops 11274289152 | bytes 31719424 | tf_op jit(solution)/shard_map/reshape | solution.py:77
  439.6 2.6 fusion.22
  442.2 25.5 %fusion.42 = (f32[8,2,512]{2,1,0:T(2,128)S(1)}, f32[8,2,512,1536]{2,3,1,0:T(8,128)}) fusion(bf16[512,8,2,128]{0,3,2,1:T(8,128)(2,1)} %fusion.22, pred[512,1536]{0,1:T(8,128)(4,1)S(1)} %copy-done.9, bf16[2,1536,8,128]{3,1,2,0:T(8,128)(2,1)} %maximum_maximum_fusion), kind=kOutput, calls=%fused_computation.85 | convolution fusion | flops 6492784128 | bytes 62423040 | tf_op jit(solution)/shard_map/sub | solution.py:104
  467.6 27.4 %fusion.10 = bf16[8,2,512,1536]{2,3,1,0:T(8,128)(2,1)} fusion(f32[8,2,512,1536]{2,3,1,0:T(8,128)} %get-tuple-element.28, f32[8,2,512]{2,1,0:T(2,128)S(1)} %get-tuple-element.27), kind=kLoop, calls=%fused_computation.14 | loop fusion | flops 25165824 | bytes 75530240 | tf_op jit(solution)/shard_map/convert_element_type | solution.py:106
  495.1 14.1 %multiply_reduce_fusion = (f32[512,8,2]{0,2,1:T(2,128)S(1)}, bf16[8,128,2,512]{3,1,2,0:T(8,128)(2,1)}) fusion(bf16[512,2048]{0,1:T(8,128)(2,1)S(1)} %copy.81, bf16[8,2,512,1536]{2,3,1,0:T(8,128)(2,1)} %fusion.10, bf16[2,1536,8,128]{3,1,2,0:T(8,128)(2,1)} %maximum_maximum_fusion), kind=kOutput, calls=%fused_computation.37 | convolution fusion | flops 3226460160 | bytes 32538624 | tf_op jit(solution)/shard_map/kgts,skd->tkgd/dot_general | solution.py:107
  509.2 14.5 %convolution_bitcast_fusion = f32[1,1536,8,128]{1,3,2,0:T(8,128)} fusion(bf16[8,2,512,1536]{2,3,1,0:T(8,128)(2,1)} %fusion.10, bf16[512,8,2,128]{0,3,2,1:T(8,128)(2,1)S(1)} %bitcast.131), kind=kOutput, calls=%fused_computation.25 | convolution fusion | flops 3221225472 | bytes 33554432 | tf_op jit(solution)/shard_map/kgts,tkgd->skd/dot_general | solution.py:115
  523.7 24.0 %fusion.13 = f32[1,1536,8,128]{1,3,2,0:T(8,128)} fusion(bf16[512,8,2,128]{0,3,2,1:T(8,128)(2,1)} %fusion.22, bf16[512,8,2,128]{0,3,2,1:T(8,128)(2,1)S(1)} %bitcast.132, f32[8,2,512]{2,1,0:T(2,128)S(1)} %bitcast.140, f32[8,2,512,1536]{2,3,1,0:T(8,128)} %get-tuple-element.28, f32[8,2,512]{2,1,0:T(2,128)S(1)} %get-tuple-element.27, ...), kind=kOutput, calls=%fused_computation.24 | convolution fusion | flops 6492782592 | bytes 64028672 | tf_op jit(solution)/shard_map/kgts,tkgd->skd/dot_general | solution.py:122
  547.7 2.7 fusion.18
  550.4 1.6 collective-permute-start.2
  552.0 11.3 %collective-permute-done.2 = bf16[2,512,8,128]{1,3,2,0:T(8,128)(2,1)S(1)} collective-permute-done((bf16[2,512,8,128]{1,3,2,0:T(8,128)(2,1)S(1)}, bf16[2,512,8,128]{1,3,2,0:T(8,128)(2,1)S(1)}, u32[]{:S(2)}, u32[]{:S(2)}) %collective-permute-start.2) | collective-permute-done | bytes 2097184 | tf_op jit(solution)/shard_map/ppermute | solution.py:19
  563.3 2.5 fusion.16
  565.8 1.6 collective-permute-start.3
  567.3 26.5 %collective-permute-done.3 = bf16[2,512,8,128]{1,3,2,0:T(8,128)(2,1)S(1)} collective-permute-done((bf16[2,512,8,128]{1,3,2,0:T(8,128)(2,1)S(1)}, bf16[2,512,8,128]{1,3,2,0:T(8,128)(2,1)S(1)}, u32[]{:S(2)}, u32[]{:S(2)}) %collective-permute-start.3) | collective-permute-done | bytes 2097184 | tf_op jit(solution)/shard_map/ppermute | solution.py:19
  597.0 19.0 %fusion.11 = bf16[5376,2048]{0,1:T(8,128)(2,1)} fusion(bf16[512,5376]{1,0:T(8,128)(2,1)} %all-gather.5.cloned.1.call-done, bf16[512,1024]{0,1:T(8,128)(2,1)S(1)} %bitcast.139, bf16[512,1024]{0,1:T(8,128)(2,1)S(1)} %fusion.34), kind=kOutput, calls=%fused_computation.15 | convolution fusion | flops 11289493504 | bytes 29622272 | tf_op jit(solution)/shard_map/dot_general | solution.py:141
  616.0 28.2 %copy.103 = bf16[5376,2048]{1,0:T(8,128)(2,1)} copy(bf16[5376,2048]{0,1:T(8,128)(2,1)} %fusion.11) | data formatting | bytes 44040192
  644.2 1.6 copy-done.1
  645.8 2.4 copy.87
  648.1 238.3 %reduce-scatter.4.cloned.1.call-done = bf16[336,2048]{1,0:T(8,128)(2,1)} async-done(((bf16[5376,2048]{1,0:T(8,128)(2,1)}), bf16[336,2048]{1,0:T(8,128)(2,1)}) %reduce-scatter.4.cloned.1.call-update) | async-done | bytes 1376272
  886.4 2.5 fusion.41
  (63 shorter events, 12.6 us)
Async XLA Ops:
  7.2 2.9 copy-start.10
  7.2 76.7 %all-gather.5.cloned.1.call-start = ((), (), s32[]{:S(2)}) async-start(), calls=%async_computation.1 | async-start | bytes 8257536 | tf_op jit(solution)/shard_map/all_gather | solution.py:61
  7.9 169.3 %all-gather.7.cloned.1.call-start = ((), (), s32[]{:S(2)}) async-start(), calls=%async_computation.2 | async-start | bytes 11698176 | tf_op jit(solution)/shard_map/all_gather | solution.py:68
  8.7 260.2 %all-gather.9.cloned.1.call-start = ((), (), s32[]{:S(2)}) async-start(), calls=%async_computation.3 | async-start | bytes 11698176 | tf_op jit(solution)/shard_map/all_gather | solution.py:69
  9.4 412.8 %all-gather.11.cloned.1.call-start = ((), (), s32[]{:S(2)}) async-start(), calls=%async_computation.4 | async-start | bytes 23396352 | tf_op jit(solution)/shard_map/all_gather | solution.py:67
  10.0 876.5 %reduce-scatter.4.cloned.1.call-start = ((), (), s32[]{:S(2)}) async-start(), calls=%async_computation.5 | async-start | bytes 23396352
  12.2 268.9 %copy-start.3 = (f32[512,128]{1,0:T(8,128)}, f32[512,128]{1,0:T(8,128)S(1)}, u32[]{:S(2)}) copy-start(f32[512,128]{1,0:T(8,128)S(1)} %get-tuple-element.32) | copy-start | bytes 786436
  279.5 2.5 copy-start.2
  280.2 1.0 copy-start.5
  282.0 73.9 %copy-start.6 = (f32[512,128]{1,0:T(8,128)S(1)}, f32[512,128]{1,0:T(8,128)}, u32[]{:S(2)}) copy-start(f32[512,128]{1,0:T(8,128)} %get-tuple-element.31) | copy-start | bytes 786436
  282.0 74.7 %copy-start.4 = (f32[512,128]{1,0:T(8,128)S(1)}, f32[512,128]{1,0:T(8,128)}, u32[]{:S(2)}) copy-start(f32[512,128]{1,0:T(8,128)} %copy-done.3) | copy-start | bytes 786436
  282.2 6.1 collective-permute-start
  288.3 74.3 %collective-permute-start.1 = (bf16[2,512,8,128]{3,1,2,0:T(8,128)(2,1)}, bf16[2,512,8,128]{3,1,2,0:T(8,128)(2,1)}, u32[]{:S(2)}, u32[]{:S(2)}) collective-permute-start(bf16[2,512,8,128]{3,1,2,0:T(8,128)(2,1)} %collective-permute-done), channel_id=1, source_target_pairs={{0,2},{2,4},{4,6},{6,8},{8,10},{10,12},{12,14},{14,16},{16,18},{18... | collective-permute-start | bytes 6291464 | tf_op jit(solution)/shard_map/ppermute | solution.py:19
  438.7 1.0 copy-start.7
  439.6 2.6 copy-start.9
  547.6 15.7 %copy-start = (f32[1,1536,8,128]{1,3,2,0:T(8,128)S(1)}, f32[1,1536,8,128]{1,3,2,0:T(8,128)}, u32[]{:S(2)}) copy-start(f32[1,1536,8,128]{1,3,2,0:T(8,128)} %fusion.13) | copy-start | bytes 18874372
  547.7 46.2 %slice-start = ((s8[6291456]{0:T(1024)(128)(4,1)}), s8[4194304]{0:T(1024)(128)(4,1)S(1)}, s32[]{:S(2)}) async-start(s8[6291456]{0:T(1024)(128)(4,1)} %bitcast.127), calls=%async_computation.6 | async-start | bytes 8388608
  550.4 43.5 %slice-start.1 = ((s8[6291456]{0:T(1024)(128)(4,1)}), s8[2097152]{0:T(1024)(128)(4,1)S(1)}, s32[]{:S(2)}) async-start(s8[6291456]{0:T(1024)(128)(4,1)} %bitcast.127), calls=%async_computation.7 | async-start | bytes 4194304
  550.4 12.9 %collective-permute-start.2 = (bf16[2,512,8,128]{1,3,2,0:T(8,128)(2,1)S(1)}, bf16[2,512,8,128]{1,3,2,0:T(8,128)(2,1)S(1)}, u32[]{:S(2)}, u32[]{:S(2)}) collective-permute-start(bf16[2,512,8,128]{1,3,2,0:T(8,128)(2,1)S(1)} %fusion.18), channel_id=1, source_target_pairs={{2,0},{4,2},{6,4},{8,6},{10,8},{12,10},{14,12},{16,14},{18,16},{20... | collective-permute-start | bytes 6291464 | tf_op jit(solution)/shard_map/ppermute | solution.py:19
  565.8 28.1 %collective-permute-start.3 = (bf16[2,512,8,128]{1,3,2,0:T(8,128)(2,1)S(1)}, bf16[2,512,8,128]{1,3,2,0:T(8,128)(2,1)S(1)}, u32[]{:S(2)}, u32[]{:S(2)}) collective-permute-start(bf16[2,512,8,128]{1,3,2,0:T(8,128)(2,1)S(1)} %fusion.16), channel_id=1, source_target_pairs={{2,0},{4,2},{6,4},{8,6},{10,8},{12,10},{14,12},{16,14},{18,16},{20... | collective-permute-start | bytes 6291464 | tf_op jit(solution)/shard_map/ppermute | solution.py:19
  595.4 1.0 copy-start.8
  644.2 1.6 copy-start.1
Sparse Core Ops, SparseCore 0:
  9.6 74.2 all-gather.4
  86.1 91.0 all-gather.6
  179.5 89.2 all-gather.8
  270.3 151.8 all-gather.10
  644.3 242.0 reduce-scatter.3
where the time goes:
time: 897 us; the launch traced here: 895 us
  waiting for transfers between devices  581 us (65%)
  matrix products  134 us (15%)
  starting transfers between devices  74.4 us (8%)
  other arithmetic  50.7 us (6%)
  local copies, waits for them, and re-layouts  41.3 us (5%)
  between operations  14.1 us (2%)
    unnamed x6, waiting for transfers between devices  241 us
    all_gather x1, waiting for transfers between devices, shards(): lax.all_gather(key_weight, 'ctx', axis=0, tiled=True)  93.4 us
    all_gather x1, waiting for transfers between devices, shards(): lax.all_gather(value_weight, 'ctx', axis=0, tiled=True)  80.9 us
    ppermute x4, starting transfers between devices, passed_along(): return lax.ppermute(block, axis, route)  74.2 us
    all_gather x1, waiting for transfers between devices, shards(): gathered = lax.all_gather(features, 'head', axis=1, tiled=True)  71.6 us
    all_gather x1, waiting for transfers between devices, shards(): lax.all_gather(query_weight, 'ctx', axis=0, tiled=True)  53.7 us
    ppermute x4, waiting for transfers between devices, passed_along(): return lax.ppermute(block, axis, route)  40.5 us
    unnamed x31, local copies, waits for them, and re-layouts  36.4 us
  transfers between devices with their start and end apart: 9, of which 8 were waited for; matrix products, arithmetic and copies ran while one was open for 5% of the time, Pallas kernels for 0%

commit v1 on v0

v1 whole, which is shorter than its diff:
```python
import jax
import jax.numpy as jnp
from jax import lax
from jax.sharding import Mesh, PartitionSpec as P

D = 5376
HEADS_Q = 32
HEAD_DIM = 128
WINDOW = 1024
SPAN = 2
CHUNKS = 4
CTX = ("chip", "core")


ROPE_BASE = 10000.0


def moved(block, distance):
    devices = range(lax.axis_size(CTX))
    route = [(i - distance, i) for i in devices if i - distance in devices]
    return lax.ppermute(block, CTX, route)


def from_partner(block, axis):
    return lax.ppermute(block, axis, [(0, 1), (1, 0)])


def rotate_half(values):
    middle = values.shape[-1] // 2
    return jnp.concatenate([-values[..., middle:], values[..., :middle]], axis=-1)


def rope_tables(offsets):
    middle = HEAD_DIM // 2
    inverse = ROPE_BASE ** (-(jnp.arange(middle).astype(jnp.float32) * 2.0 / HEAD_DIM))
    angles = offsets.astype(jnp.float32)[:, None] * inverse[None, :]
    cosine = jnp.cos(angles)
    sine_table = jnp.sin(angles)
    return (
        jnp.concatenate([cosine, cosine], axis=-1),
        jnp.concatenate([sine_table, sine_table], axis=-1),
    )


def rotate(values, cosine, sine_table):
    return values * cosine[:, None, :] + rotate_half(values) * sine_table[:, None, :]


def unrotate(values, cosine, sine_table):
    return values * cosine[:, None, :] - rotate_half(values) * sine_table[:, None, :]


def start_of(positions, starts):
    candidates = jnp.where(starts[None, :] <= positions[:, None], starts[None, :], -1)
    return jnp.max(candidates, axis=1)


def gather_features(features):
    if lax.axis_size("head") != 2:
        return lax.all_gather(features, "head", axis=1, tiled=True)
    mine = lax.axis_index("head") * features.shape[1]
    whole = jnp.zeros((features.shape[0], 2 * features.shape[1]), features.dtype)
    whole = lax.dynamic_update_slice(whole, features, (0, mine))
    return lax.dynamic_update_slice(
        whole, from_partner(features, "head"), (0, features.shape[1] - mine)
    )


def attend(grouped, key_block, value_block, grad_heads, allowed):
    scores = jnp.einsum("tkgd,skd->kgts", grouped, key_block, preferred_element_type=jnp.float32)
    row_max = jnp.max(jnp.where(allowed, scores, -jnp.inf), axis=-1, keepdims=True)
    raw_weights = jnp.where(allowed, jnp.exp(scores - row_max), 0.0)
    prob_soft = raw_weights / jnp.sum(raw_weights, axis=-1, keepdims=True)
    probs_low = prob_soft.astype(jnp.bfloat16)
    attended = jnp.einsum(
        "kgts,skd->tkgd", probs_low, value_block, preferred_element_type=jnp.float32
    ).astype(jnp.bfloat16)
    out_dot = jnp.sum(
        grad_heads.astype(jnp.float32) * attended.astype(jnp.float32), axis=-1
    ).transpose(1, 2, 0)[..., None]
    value_partial = jnp.einsum(
        "kgts,tkgd->skd", probs_low, grad_heads, preferred_element_type=jnp.float32
    )
    prob_grad = jnp.einsum(
        "tkgd,skd->kgts", grad_heads, value_block, preferred_element_type=jnp.float32
    )
    score_grad = (prob_soft * (prob_grad - out_dot)).astype(jnp.bfloat16)
    key_partial = jnp.einsum(
        "kgts,tkgd->skd", score_grad, grouped, preferred_element_type=jnp.float32
    )
    return attended, key_partial, value_partial


def shards(features, query_weight, key_weight, value_weight, doc_lengths, out_grad):
    tok_rows = features.shape[0]
    query_cols = query_weight.shape[1]
    value_cols = key_weight.shape[1]
    query_heads = query_cols // HEAD_DIM
    value_heads = value_cols // HEAD_DIM
    group_size = query_heads // value_heads
    query_scale = (D / HEADS_Q) ** (-0.5)
    chunks = min(CHUNKS, value_heads)
    chunk_heads = value_heads // chunks
    chunk_cols = value_cols // chunks
    ctx_index = lax.axis_index(CTX)
    core = lax.axis_index("core")

    def gathered_rows(piece):
        mine = lax.all_gather(piece, "chip", axis=0, tiled=True)
        return mine, from_partner(mine, "core")

    def projected(rows):
        mine, other = rows
        return jnp.dot(kept, mine, preferred_element_type=jnp.float32) + jnp.dot(
            given, other, preferred_element_type=jnp.float32
        )

    pair = min(2, chunks)
    kv_weights, q_weights = [], []
    for first in range(0, chunks, pair):
        cols = slice(first * chunk_cols, (first + pair) * chunk_cols)
        kv_weights.append(
            gathered_rows(jnp.concatenate([key_weight[:, cols], value_weight[:, cols]], axis=1))
        )
        for chunk in range(first, first + pair):
            width = chunk_cols * group_size
            q_weights.append(gathered_rows(query_weight[:, chunk * width : (chunk + 1) * width]))

    gathered = gather_features(features)
    chips = lax.axis_size("chip")
    by_core = gathered.reshape(tok_rows, chips, 2, D // (2 * chips))
    kept = lax.dynamic_index_in_dim(by_core, core, 2, keepdims=False).reshape(tok_rows, D // 2)
    given = lax.dynamic_index_in_dim(by_core, 1 - core, 2, keepdims=False).reshape(tok_rows, D // 2)
    chip_features = jnp.concatenate([kept, from_partner(given, "core")], axis=0)

    starts = jnp.cumsum(doc_lengths) - doc_lengths
    query_index = ctx_index * tok_rows + jnp.arange(tok_rows, dtype=jnp.int32)
    query_start = start_of(query_index, starts)
    cosine, sine_table = rope_tables(query_index - query_start)
    key_rows = (SPAN + 1) * tok_rows
    key_index = (ctx_index - SPAN) * tok_rows + jnp.arange(key_rows, dtype=jnp.int32)
    key_start = start_of(key_index, starts)
    offsets_qk = query_index[:, None] - key_index[None, :]
    allowed = (
        (key_index[None, :] >= 0)
        & (offsets_qk >= 0)
        & (offsets_qk < WINDOW)
        & (query_start[:, None] == key_start[None, :])
    )

    blocks = []
    for weights in kv_weights:
        proj = projected(weights)
        half = proj.shape[1] // 2
        own_keys = rotate(proj[:, :half].reshape(tok_rows, -1, HEAD_DIM), cosine, sine_table)
        own_values = proj[:, half:].reshape(tok_rows, -1, HEAD_DIM)
        key_value = jnp.stack([own_keys, own_values]).astype(jnp.bfloat16)
        earlier = []
        moving = key_value
        for distance in range(1, SPAN + 1):
            moving = moved(moving, 1)
            earlier.insert(0, moving)
        blocks.append(jnp.concatenate(earlier + [key_value], axis=1))

    attended, key_sums, value_sums = [], [], []
    for chunk in range(chunks):
        width = chunk_cols * group_size
        proj = projected(q_weights[chunk])
        grouped = (
            (rotate(proj.reshape(tok_rows, -1, HEAD_DIM), cosine, sine_table) * query_scale)
            .astype(jnp.bfloat16)
            .reshape(tok_rows, chunk_heads, group_size, HEAD_DIM)
        )
        at = chunk % pair
        block = blocks[chunk // pair][:, :, at * chunk_heads : (at + 1) * chunk_heads]
        grad_heads = out_grad[:, chunk * width : (chunk + 1) * width].reshape(
            tok_rows, chunk_heads, group_size, HEAD_DIM
        )
        out, key_partial, value_partial = attend(grouped, block[0], block[1], grad_heads, allowed)
        attended.append(out.reshape(tok_rows, width))
        partials = jnp.stack([key_partial, value_partial])

        def piece_of(distance):
            return partials[:, (SPAN - distance) * tok_rows : (SPAN - distance + 1) * tok_rows]

        returned = piece_of(SPAN)
        for distance in range(SPAN, 0, -1):
            returned = moved(returned.astype(jnp.bfloat16), -1).astype(jnp.float32) + piece_of(
                distance - 1
            )
        key_grad = unrotate(returned[0], cosine, sine_table).astype(jnp.bfloat16)
        value_grad = returned[1].astype(jnp.bfloat16)
        pair_grads = jnp.concatenate(
            [key_grad.reshape(tok_rows, chunk_cols), value_grad.reshape(tok_rows, chunk_cols)],
            axis=1,
        )
        chip_grads = jnp.concatenate([pair_grads, from_partner(pair_grads, "core")], axis=0)
        term = lax.dot_general(
            chip_features, chip_grads, (((0,), (0,)), ((), ())), preferred_element_type=jnp.float32
        ).astype(jnp.bfloat16)
        summed = lax.psum_scatter(term, "chip", scatter_dimension=0, tiled=True)
        key_sums.append(summed[:, :chunk_cols])
        value_sums.append(summed[:, chunk_cols:])
    return (
        jnp.concatenate(attended, axis=1),
        jnp.concatenate(key_sums, axis=1),
        jnp.concatenate(value_sums, axis=1),
    )


def solution(mesh):
    ctx, head = mesh.shape["ctx"], mesh.shape["head"]
    split = Mesh(mesh.devices.reshape(ctx // 2, 2, head), ("chip", "core", "head"))
    placed = P(CTX, "head")
    return jax.shard_map(
        shards,
        mesh=split,
        in_specs=(placed, placed, placed, placed, P(), placed),
        out_specs=(placed, placed, placed),
        check_vma=False,
    )
```

time: 897 us -> 1040 us (1.16)
  waiting for transfers between devices: 581 us -> 643 us
  matrix products: 134 us -> 187 us
  local copies, waits for them, and re-layouts: 41.3 us -> 71.4 us
  starting transfers between devices: 74.4 us -> 52 us
    reduce_scatter x0 -> x4, waiting for transfers between devices: none -> 260 us  [shards(): summed = lax.psum_scatter(term, 'chip', scatter_dimension=0, tiled=True)]
    unnamed x6 -> x10, waiting for transfers between devices: 241 us -> 1.84 us
    all_gather x4 -> x6, waiting for transfers between devices: 300 us -> 362 us  [gathered_rows(): mine = lax.all_gather(piece, 'chip', axis=0, tiled=True)]
    dot_general x6 -> x28, matrix products: 92 us -> 148 us  [the longest x4 35.9 us: attend(): jnp.einsum('kgts,tkgd->skd', score_grad, grouped, preferred_element_type=...]
    slice x3 -> x25, local copies, waits for them, and re-layouts: 3.13 us -> 28.9 us  [the longest x5 11.4 us: shards(): out_grad[:, chunk * width:(chunk + 1) * width]]
    unnamed x31 -> x140, local copies, waits for them, and re-layouts: 36.4 us -> 13.3 us
    ppermute x4 -> x24, starting transfers between devices: 74.2 us -> 51.4 us  [the longest x12 28.1 us: moved(): return lax.ppermute(block, CTX, route)]
    ppermute x4 -> x24, waiting for transfers between devices: 40.5 us -> 19.7 us  [the longest x12 13.6 us: moved(): return lax.ppermute(block, CTX, route)]
  transfers between devices with their start and end apart: 9 -> 34, of which waited for: 8 -> 19; matrix products, arithmetic and copies ran while one was open for 5% -> 29% of each run, Pallas kernels for 0% -> 0%
where the time goes in v1:
time: 1040 us; the launch traced here: 1030 us
  waiting for transfers between devices  643 us (62%)
  matrix products  187 us (18%)
  local copies, waits for them, and re-layouts  71.4 us (7%)
  other arithmetic  60.3 us (6%)
  starting transfers between devices  52 us (5%)
  between operations  15.8 us (2%)
    all_gather x6, waiting for transfers between devices, gathered_rows(): mine = lax.all_gather(piece, 'chip', axis=0, tiled=True)  362 us
    reduce_scatter x4, waiting for transfers between devices, shards(): summed = lax.psum_scatter(term, 'chip', scatter_dimension=0, tiled=True)  260 us
    sub x4, matrix products, attend(): raw_weights = jnp.where(allowed, jnp.exp(scores - row_max), 0.0)  39.3 us
    dot_general x4, matrix products, attend(): jnp.einsum('kgts,tkgd->skd', score_grad, grouped, preferred_element_type=...  35.9 us
    dot_general x6, matrix products, projected(): jnp.dot(given, other, preferred_element_type=jnp.float32)  34 us
    ppermute x12, starting transfers between devices, moved(): return lax.ppermute(block, CTX, route)  28.1 us
    convert_element_type x4, other arithmetic, attend(): probs_low = prob_soft.astype(jnp.bfloat16)  25.6 us
    dot_general x4, matrix products, shards(): lax.dot_general(chip_features, chip_grads, (((0,), (0,)), ((), ())), pref...  25.6 us
  transfers between devices with their start and end apart: 34, of which 19 were waited for; matrix products, arithmetic and copies ran while one was open for 29% of the time, Pallas kernels for 0%

profile of v1, /device:TPU:0, one launch (start us, length us, event | category | flops | bytes accessed | tf_op | source)
XLA Modules:
  0.0 1029.9 jit_solution(1405364824924042498)
XLA Ops:
  20.5 49.4 %all-gather.17.cloned.1.call-done = bf16[2688,512]{1,0:T(8,128)(2,1)} async-done(((bf16[336,512]{1,0:T(8,128)(2,1)}), bf16[2688,512]{1,0:T(8,128)(2,1)}) %all-gather.17.cloned.1.call-update) | async-done | bytes 2752528 | tf_op jit(solution)/shard_map/all_gather | solution.py:109
  69.9 90.8 %all-gather.7.cloned.1.call-done = bf16[2688,1024]{1,0:T(8,128)(2,1)} async-done(((bf16[336,1024]{1,0:T(8,128)(2,1)}), bf16[2688,1024]{1,0:T(8,128)(2,1)}) %all-gather.7.cloned.1.call-update) | async-done | bytes 5505040 | tf_op jit(solution)/shard_map/all_gather | solution.py:109
  162.4 54.7 %all-gather.15.cloned.1.call-done = bf16[2688,512]{1,0:T(8,128)(2,1)} async-done(((bf16[336,512]{1,0:T(8,128)(2,1)}), bf16[2688,512]{1,0:T(8,128)(2,1)}) %all-gather.15.cloned.1.call-update) | async-done | bytes 2752528 | tf_op jit(solution)/shard_map/all_gather | solution.py:109
  221.5 52.4 %all-gather.11.cloned.1.call-done = bf16[2688,512]{1,0:T(8,128)(2,1)} async-done(((bf16[336,512]{1,0:T(8,128)(2,1)}), bf16[2688,512]{1,0:T(8,128)(2,1)}) %all-gather.11.cloned.1.call-update) | async-done | bytes 2752528 | tf_op jit(solution)/shard_map/all_gather | solution.py:109
  291.8 72.7 %all-gather.13.cloned.1.call-done = bf16[2688,1024]{1,0:T(8,128)(2,1)} async-done(((bf16[336,1024]{1,0:T(8,128)(2,1)}), bf16[2688,1024]{1,0:T(8,128)(2,1)}) %all-gather.13.cloned.1.call-update) | async-done | bytes 5505040 | tf_op jit(solution)/shard_map/all_gather | solution.py:109
  373.1 5.8 fusion.151
  378.8 42.0 %all-gather.9.cloned.1.call-done = bf16[2688,512]{1,0:T(8,128)(2,1)} async-done(((bf16[336,512]{1,0:T(8,128)(2,1)}), bf16[2688,512]{1,0:T(8,128)(2,1)}) %all-gather.9.cloned.1.call-update) | async-done | bytes 2752528 | tf_op jit(solution)/shard_map/all_gather | solution.py:109
  437.9 6.5 fusion.146
  447.7 8.6 fusion.149
  462.5 6.4 convolution_add_fusion
  517.4 8.6 collective-permute-start.3
  527.3 9.6 fusion.143
  536.9 6.4 fusion.42
  547.5 8.9 convolution_bitcast_fusion.3
  566.2 9.6 fusion.144
  575.7 6.4 fusion.41
  588.7 9.0 convolution_bitcast_fusion.5
  600.4 10.1 fusion.145
  610.5 6.4 fusion.40
  623.4 9.0 convolution_bitcast_fusion.7
  634.8 10.1 fusion.142
  644.9 6.4 fusion.43
  655.5 9.0 convolution_bitcast_fusion.1
  698.3 18.5 %collective-permute-start.14 = (bf16[512,512]{0,1:T(8,128)(2,1)S(1)}, bf16[512,512]{0,1:T(8,128)(2,1)S(1)}, u32[]{:S(2)}, u32[]{:S(2)}) collective-permute-start(bf16[512,512]{0,1:T(8,128)(2,1)S(1)} %pad_maximum_fusion.12), channel_id=1, source_target_pairs={{0,2},{2,0},{1,3},{3,1},{4,6},{6,4},{5,7},{7,5},{8,10},{10,8},{9,1... | collective-permute-start | bytes 1572872 | tf_op jit(solution)/shard_map/ppermute | solution.py:25
  718.3 6.4 convolution_convert_fusion.3
  727.8 6.4 convolution_convert_fusion.2
  737.4 6.4 convolution_convert_fusion.1
  747.2 6.4 convolution_convert_fusion
  757.0 42.0 %reduce-scatter.5.cloned.1.call-done = bf16[336,512]{1,0:T(8,128)(2,1)} async-done(((bf16[2688,512]{1,0:T(8,128)(2,1)}), bf16[336,512]{1,0:T(8,128)(2,1)}) %reduce-scatter.5.cloned.1.call-update) | async-done | bytes 344080 | tf_op jit(solution)/shard_map/reduce_scatter | solution.py:201
  800.1 72.6 %reduce-scatter.7.cloned.1.call-done = bf16[336,512]{1,0:T(8,128)(2,1)} async-done(((bf16[2688,512]{1,0:T(8,128)(2,1)}), bf16[336,512]{1,0:T(8,128)(2,1)}) %reduce-scatter.7.cloned.1.call-update) | async-done | bytes 344080 | tf_op jit(solution)/shard_map/reduce_scatter | solution.py:201
  873.7 73.0 %reduce-scatter.9.cloned.1.call-done = bf16[336,512]{1,0:T(8,128)(2,1)} async-done(((bf16[2688,512]{1,0:T(8,128)(2,1)}), bf16[336,512]{1,0:T(8,128)(2,1)}) %reduce-scatter.9.cloned.1.call-update) | async-done | bytes 344080 | tf_op jit(solution)/shard_map/reduce_scatter | solution.py:201
  947.7 72.2 %reduce-scatter.11.cloned.1.call-done = bf16[336,512]{1,0:T(8,128)(2,1)} async-done(((bf16[2688,512]{1,0:T(8,128)(2,1)}), bf16[336,512]{1,0:T(8,128)(2,1)}) %reduce-scatter.11.cloned.1.call-update) | async-done | bytes 344080 | tf_op jit(solution)/shard_map/reduce_scatter | solution.py:201
  (317 shorter events, 211.5 us)
Async XLA Ops:
  7.2 62.7 %all-gather.17.cloned.1.call-start = ((), (), s32[]{:S(2)}) async-start(), calls=%async_computation.9 | async-start | bytes 3096576 | tf_op jit(solution)/shard_map/all_gather | solution.py:109
  9.8 150.9 %all-gather.7.cloned.1.call-start = ((), (), s32[]{:S(2)}) async-start(), calls=%async_computation.4 | async-start | bytes 6193152 | tf_op jit(solution)/shard_map/all_gather | solution.py:109
  10.9 206.2 %all-gather.15.cloned.1.call-start = ((), (), s32[]{:S(2)}) async-start(), calls=%async_computation.8 | async-start | bytes 3096576 | tf_op jit(solution)/shard_map/all_gather | solution.py:109
  11.7 262.2 %all-gather.11.cloned.1.call-start = ((), (), s32[]{:S(2)}) async-start(), calls=%async_computation.6 | async-start | bytes 3096576 | tf_op jit(solution)/shard_map/all_gather | solution.py:109
  12.2 352.3 %all-gather.13.cloned.1.call-start = ((), (), s32[]{:S(2)}) async-start(), calls=%async_computation.7 | async-start | bytes 6193152 | tf_op jit(solution)/shard_map/all_gather | solution.py:109
  13.3 407.6 %all-gather.9.cloned.1.call-start = ((), (), s32[]{:S(2)}) async-start(), calls=%async_computation.5 | async-start | bytes 3096576 | tf_op jit(solution)/shard_map/all_gather | solution.py:109
  13.8 785.2 %reduce-scatter.5.cloned.1.call-start = ((), (), s32[]{:S(2)}) async-start(), calls=%async_computation.10 | async-start | bytes 3096576 | tf_op jit(solution)/shard_map/reduce_scatter | solution.py:201
  17.2 274.6 %collective-permute-start = (bf16[512,2688]{0,1:T(8,128)(2,1)S(1)}, bf16[512,2688]{0,1:T(8,128)(2,1)}, u32[]{:S(2)}, u32[]{:S(2)}) collective-permute-start(bf16[512,2688]{0,1:T(8,128)(2,1)S(1)} %copy.90), channel_id=1, source_target_pairs={{0,1},{1,0},{2,3},{3,2},{4,5},{5,4},{6,7},{7,6},{8,9},{9,8},{10,11... | collective-permute-start | bytes 8257544 | tf_op jit(solution)/shard_map/ppermute | solution.py:25
  69.8 302.7 %collective-permute-start.10 = (bf16[2688,512]{1,0:T(8,128)(2,1)}, bf16[2688,512]{1,0:T(8,128)(2,1)}, u32[]{:S(2)}, u32[]{:S(2)}) collective-permute-start(bf16[2688,512]{1,0:T(8,128)(2,1)} %all-gather.17.cloned.1.call-done), channel_id=1, source_target_pairs={{0,2},{2,0},{1,3},{3,1},{4,6},{6,4},{5,7},{7,5},{8,10},{10,8},{9,1... | collective-permute-start | bytes 8257544 | tf_op jit(solution)/shard_map/ppermute | solution.py:25
  160.7 277.3 %collective-permute-start.1 = (bf16[2688,1024]{1,0:T(8,128)(2,1)}, bf16[2688,1024]{1,0:T(8,128)(2,1)}, u32[]{:S(2)}, u32[]{:S(2)}) collective-permute-start(bf16[2688,1024]{1,0:T(8,128)(2,1)} %all-gather.7.cloned.1.call-done), channel_id=1, source_target_pairs={{0,2},{2,0},{1,3},{3,1},{4,6},{6,4},{5,7},{7,5},{8,10},{10,8},{9,1... | collective-permute-start | bytes 16515080 | tf_op jit(solution)/shard_map/ppermute | solution.py:25
  217.1 203.7 %collective-permute-start.9 = (bf16[2688,512]{1,0:T(8,128)(2,1)}, bf16[2688,512]{1,0:T(8,128)(2,1)}, u32[]{:S(2)}, u32[]{:S(2)}) collective-permute-start(bf16[2688,512]{1,0:T(8,128)(2,1)} %all-gather.15.cloned.1.call-done), channel_id=1, source_target_pairs={{0,2},{2,0},{1,3},{3,1},{4,6},{6,4},{5,7},{7,5},{8,10},{10,8},{9,1... | collective-permute-start | bytes 8257544 | tf_op jit(solution)/shard_map/ppermute | solution.py:25
  273.8 151.3 %collective-permute-start.5 = (bf16[2688,512]{1,0:T(8,128)(2,1)}, bf16[2688,512]{1,0:T(8,128)(2,1)}, u32[]{:S(2)}, u32[]{:S(2)}) collective-permute-start(bf16[2688,512]{1,0:T(8,128)(2,1)} %all-gather.11.cloned.1.call-done), channel_id=1, source_target_pairs={{0,2},{2,0},{1,3},{3,1},{4,6},{6,4},{5,7},{7,5},{8,10},{10,8},{9,1... | collective-permute-start | bytes 8257544 | tf_op jit(solution)/shard_map/ppermute | solution.py:25
  364.5 83.2 %collective-permute-start.6 = (bf16[2688,1024]{1,0:T(8,128)(2,1)}, bf16[2688,1024]{1,0:T(8,128)(2,1)}, u32[]{:S(2)}, u32[]{:S(2)}) collective-permute-start(bf16[2688,1024]{1,0:T(8,128)(2,1)} %all-gather.13.cloned.1.call-done), channel_id=1, source_target_pairs={{0,2},{2,0},{1,3},{3,1},{4,6},{6,4},{5,7},{7,5},{8,10},{10,8},{9,1... | collective-permute-start | bytes 16515080 | tf_op jit(solution)/shard_map/ppermute | solution.py:25
  372.6 344.2 %collective-permute-start.11 = (bf16[512,2688]{0,1:T(8,128)(2,1)}, bf16[512,2688]{0,1:T(8,128)(2,1)}, u32[]{:S(2)}, u32[]{:S(2)}) collective-permute-start(bf16[512,2688]{0,1:T(8,128)(2,1)} %bitcast.2), channel_id=1, source_target_pairs={{0,2},{2,0},{1,3},{3,1},{4,6},{6,4},{5,7},{7,5},{8,10},{10,8},{9,1... | collective-permute-start | bytes 8257544 | tf_op jit(solution)/shard_map/ppermute | solution.py:25
  420.8 77.1 %collective-permute-start.4 = (bf16[2688,512]{1,0:T(8,128)(2,1)}, bf16[2688,512]{1,0:T(8,128)(2,1)}, u32[]{:S(2)}, u32[]{:S(2)}) collective-permute-start(bf16[2688,512]{1,0:T(8,128)(2,1)} %all-gather.9.cloned.1.call-done), channel_id=1, source_target_pairs={{0,2},{2,0},{1,3},{3,1},{4,6},{6,4},{5,7},{7,5},{8,10},{10,8},{9,1... | collective-permute-start | bytes 8257544 | tf_op jit(solution)/shard_map/ppermute | solution.py:25
  494.1 17.9 %collective-permute-start.7 = (bf16[2,512,4,128]{3,1,2,0:T(8,128)(2,1)}, bf16[2,512,4,128]{3,1,2,0:T(8,128)(2,1)}, u32[]{:S(2)}, u32[]{:S(2)}) collective-permute-start(bf16[2,512,4,128]{3,1,2,0:T(8,128)(2,1)} %pad_maximum_fusion.7), channel_id=1, source_target_pairs={{0,2},{2,4},{4,6},{6,8},{8,10},{10,12},{12,14},{14,16},{16,18},{18... | collective-permute-start | bytes 3145736 | tf_op jit(solution)/shard_map/ppermute | solution.py:21
  509.6 7.8 collective-permute-start.2
  512.0 14.0 %collective-permute-start.8 = (bf16[2,512,4,128]{3,1,2,0:T(8,128)(2,1)}, bf16[2,512,4,128]{3,1,2,0:T(8,128)(2,1)S(1)}, u32[]{:S(2)}, u32[]{:S(2)}) collective-permute-start(bf16[2,512,4,128]{3,1,2,0:T(8,128)(2,1)} %collective-permute-done.7), channel_id=1, source_target_pairs={{0,2},{2,4},{4,6},{6,8},{8,10},{10,12},{12,14},{14,16},{16,18},{18... | collective-permute-start | bytes 3145736 | tf_op jit(solution)/shard_map/ppermute | solution.py:21
  517.4 47.1 %collective-permute-start.3 = (bf16[2,512,4,128]{3,1,2,0:T(8,128)(2,1)}, bf16[2,512,4,128]{3,1,2,0:T(8,128)(2,1)}, u32[]{:S(2)}, u32[]{:S(2)}) collective-permute-start(bf16[2,512,4,128]{3,1,2,0:T(8,128)(2,1)} %collective-permute-done.2), channel_id=1, source_target_pairs={{0,2},{2,4},{4,6},{6,8},{8,10},{10,12},{12,14},{14,16},{16,18},{18... | collective-permute-start | bytes 3145736 | tf_op jit(solution)/shard_map/ppermute | solution.py:21
  562.8 108.3 %collective-permute-start.18 = (bf16[2,512,2,128]{1,3,2,0:T(8,128)(2,1)}, bf16[2,512,2,128]{1,3,2,0:T(8,128)(2,1)}, u32[]{:S(2)}, u32[]{:S(2)}) collective-permute-start(bf16[2,512,2,128]{1,3,2,0:T(8,128)(2,1)} %fusion.56), channel_id=1, source_target_pairs={{2,0},{4,2},{6,4},{8,6},{10,8},{12,10},{14,12},{16,14},{18,16},{20... | collective-permute-start | bytes 1572872 | tf_op jit(solution)/shard_map/ppermute | solution.py:21
  598.7 75.4 %collective-permute-start.15 = (bf16[2,512,2,128]{1,3,2,0:T(8,128)(2,1)}, bf16[2,512,2,128]{1,3,2,0:T(8,128)(2,1)}, u32[]{:S(2)}, u32[]{:S(2)}) collective-permute-start(bf16[2,512,2,128]{1,3,2,0:T(8,128)(2,1)} %fusion.61), channel_id=1, source_target_pairs={{2,0},{4,2},{6,4},{8,6},{10,8},{12,10},{14,12},{16,14},{18,16},{20... | collective-permute-start | bytes 1572872 | tf_op jit(solution)/shard_map/ppermute | solution.py:21
  633.4 43.2 %collective-permute-start.12 = (bf16[2,512,2,128]{1,3,2,0:T(8,128)(2,1)}, bf16[2,512,2,128]{1,3,2,0:T(8,128)(2,1)}, u32[]{:S(2)}, u32[]{:S(2)}) collective-permute-start(bf16[2,512,2,128]{1,3,2,0:T(8,128)(2,1)} %fusion.66), channel_id=1, source_target_pairs={{2,0},{4,2},{6,4},{8,6},{10,8},{12,10},{14,12},{16,14},{18,16},{20... | collective-permute-start | bytes 1572872 | tf_op jit(solution)/shard_map/ppermute | solution.py:21
  669.6 13.9 %collective-permute-start.21 = (bf16[2,512,2,128]{1,3,2,0:T(8,128)(2,1)S(1)}, bf16[2,512,2,128]{1,3,2,0:T(8,128)(2,1)S(1)}, u32[]{:S(2)}, u32[]{:S(2)}) collective-permute-start(bf16[2,512,2,128]{1,3,2,0:T(8,128)(2,1)S(1)} %fusion.51), channel_id=1, source_target_pairs={{2,0},{4,2},{6,4},{8,6},{10,8},{12,10},{14,12},{16,14},{18,16},{20... | collective-permute-start | bytes 1572872 | tf_op jit(solution)/shard_map/ppermute | solution.py:21
  672.5 14.5 %collective-permute-start.19 = (bf16[2,512,2,128]{1,3,2,0:T(8,128)(2,1)S(1)}, bf16[2,512,2,128]{1,3,2,0:T(8,128)(2,1)S(1)}, u32[]{:S(2)}, u32[]{:S(2)}) collective-permute-start(bf16[2,512,2,128]{1,3,2,0:T(8,128)(2,1)S(1)} %fusion.54), channel_id=1, source_target_pairs={{2,0},{4,2},{6,4},{8,6},{10,8},{12,10},{14,12},{16,14},{18,16},{20... | collective-permute-start | bytes 1572872 | tf_op jit(solution)/shard_map/ppermute | solution.py:21
  675.3 14.9 %collective-permute-start.16 = (bf16[2,512,2,128]{1,3,2,0:T(8,128)(2,1)S(1)}, bf16[2,512,2,128]{1,3,2,0:T(8,128)(2,1)S(1)}, u32[]{:S(2)}, u32[]{:S(2)}) collective-permute-start(bf16[2,512,2,128]{1,3,2,0:T(8,128)(2,1)S(1)} %fusion.59), channel_id=1, source_target_pairs={{2,0},{4,2},{6,4},{8,6},{10,8},{12,10},{14,12},{16,14},{18,16},{20... | collective-permute-start | bytes 1572872 | tf_op jit(solution)/shard_map/ppermute | solution.py:21
  677.8 15.5 %collective-permute-start.13 = (bf16[2,512,2,128]{1,3,2,0:T(8,128)(2,1)S(1)}, bf16[2,512,2,128]{1,3,2,0:T(8,128)(2,1)S(1)}, u32[]{:S(2)}, u32[]{:S(2)}) collective-permute-start(bf16[2,512,2,128]{1,3,2,0:T(8,128)(2,1)S(1)} %fusion.64), channel_id=1, source_target_pairs={{2,0},{4,2},{6,4},{8,6},{10,8},{12,10},{14,12},{16,14},{18,16},{20... | collective-permute-start | bytes 1572872 | tf_op jit(solution)/shard_map/ppermute | solution.py:21
  683.7 11.7 %collective-permute-start.22 = (bf16[2,512,2,128]{1,3,2,0:T(8,128)(2,1)S(1)}, bf16[2,512,2,128]{1,3,2,0:T(8,128)(2,1)S(1)}, u32[]{:S(2)}, u32[]{:S(2)}) collective-permute-start(bf16[2,512,2,128]{1,3,2,0:T(8,128)(2,1)S(1)} %fusion.49), channel_id=1, source_target_pairs={{2,0},{4,2},{6,4},{8,6},{10,8},{12,10},{14,12},{16,14},{18,16},{20... | collective-permute-start | bytes 1572872 | tf_op jit(solution)/shard_map/ppermute | solution.py:21
  698.3 20.0 %collective-permute-start.14 = (bf16[512,512]{0,1:T(8,128)(2,1)S(1)}, bf16[512,512]{0,1:T(8,128)(2,1)S(1)}, u32[]{:S(2)}, u32[]{:S(2)}) collective-permute-start(bf16[512,512]{0,1:T(8,128)(2,1)S(1)} %pad_maximum_fusion.12), channel_id=1, source_target_pairs={{0,2},{2,0},{1,3},{3,1},{4,6},{6,4},{5,7},{7,5},{8,10},{10,8},{9,1... | collective-permute-start | bytes 1572872 | tf_op jit(solution)/shard_map/ppermute | solution.py:25
  724.7 148.0 %reduce-scatter.7.cloned.1.call-start = ((), (), s32[]{:S(2)}) async-start(), calls=%async_computation.11 | async-start | bytes 3096576 | tf_op jit(solution)/shard_map/reduce_scatter | solution.py:201
  734.3 212.4 %reduce-scatter.9.cloned.1.call-start = ((), (), s32[]{:S(2)}) async-start(), calls=%async_computation.12 | async-start | bytes 3096576 | tf_op jit(solution)/shard_map/reduce_scatter | solution.py:201
  735.4 2.0 collective-permute-start.20
  743.8 276.1 %reduce-scatter.11.cloned.1.call-start = ((), (), s32[]{:S(2)}) async-start(), calls=%async_computation.13 | async-start | bytes 3096576 | tf_op jit(solution)/shard_map/reduce_scatter | solution.py:201
  (70 other events, 1020.0 us)
Sparse Core Ops, SparseCore 0:
  10.8 59.0 all-gather.16
  72.6 88.0 all-gather.6
  162.9 54.2 all-gather.14
  219.2 54.6 all-gather.10
  276.4 88.0 all-gather.12
  366.6 54.2 all-gather.8
  724.8 74.2 reduce-scatter.4
  802.6 70.0 reduce-scatter.6
  876.2 70.4 reduce-scatter.8
  950.1 69.7 reduce-scatter.10

commit v2 on v1

v2 whole, which is shorter than its diff:
```python
import functools

import jax
import jax.numpy as jnp
from jax import lax
from jax.experimental import pallas as pl
from jax.experimental.pallas import tpu as pltpu
from jax.sharding import Mesh, PartitionSpec as P

D = 5376
HEADS_Q = 32
HEAD_DIM = 128
WINDOW = 1024
SPAN = 2
CTX = ("chip", "core")


ROPE_BASE = 10000.0


def moved(block, distance):
    devices = range(lax.axis_size(CTX))
    route = [(i - distance, i) for i in devices if i - distance in devices]
    return lax.ppermute(block, CTX, route)


def from_partner(block, axis):
    return lax.ppermute(block, axis, [(0, 1), (1, 0)])


def ring_of(chips):
    return list(range(0, chips, 2)) + list(range(chips - 1, 0, -2))


def along_ring(block, step):
    ring = ring_of(lax.axis_size("chip"))
    route = [(ring[i], ring[(i + step) % len(ring)]) for i in range(len(ring))]
    return lax.ppermute(block, "chip", route)


def ring_gather(shard):
    chips = lax.axis_size("chip")
    half = shard.shape[1] // 2
    found = {0: shard}
    ahead = behind = shard
    for step in range(1, chips // 2):
        behind, ahead = along_ring(behind, 1), along_ring(ahead, -1)
        found[step], found[chips - step] = ahead, behind
    found[chips // 2] = jnp.concatenate(
        [along_ring(behind[:, :half], 1), along_ring(ahead[:, half:], -1)], axis=1
    )
    return found


def ring_scatter(term):
    chips = lax.axis_size("chip")
    farthest = term(chips // 2).astype(jnp.bfloat16)
    half = farthest.shape[1] // 2
    onward, back = along_ring(farthest[:, :half], 1), along_ring(farthest[:, half:], -1)
    onward = jnp.pad(onward, ((0, 0), (0, half)))
    back = jnp.pad(back, ((0, 0), (half, 0)))
    for step in range(chips // 2 - 1, 0, -1):
        onward = along_ring((term(step) + onward.astype(jnp.float32)).astype(jnp.bfloat16), 1)
        back = along_ring((term(chips - step) + back.astype(jnp.float32)).astype(jnp.bfloat16), -1)
    return term(0) + onward.astype(jnp.float32) + back.astype(jnp.float32)


def rotate_half(values):
    middle = values.shape[-1] // 2
    return jnp.concatenate([-values[..., middle:], values[..., :middle]], axis=-1)


def rope_tables(offsets):
    middle = HEAD_DIM // 2
    inverse = ROPE_BASE ** (-(jnp.arange(middle).astype(jnp.float32) * 2.0 / HEAD_DIM))
    angles = offsets.astype(jnp.float32)[:, None] * inverse[None, :]
    cosine = jnp.cos(angles)
    sine_table = jnp.sin(angles)
    return (
        jnp.concatenate([cosine, cosine], axis=-1),
        jnp.concatenate([sine_table, sine_table], axis=-1),
    )


def rotate(values, cosine, sine_table):
    return values * cosine[:, None, :] + rotate_half(values) * sine_table[:, None, :]


def unrotate(values, cosine, sine_table):
    return values * cosine[:, None, :] - rotate_half(values) * sine_table[:, None, :]


def start_of(positions, starts):
    candidates = jnp.where(starts[None, :] <= positions[:, None], starts[None, :], -1)
    return jnp.max(candidates, axis=1)


def gather_features(features):
    if lax.axis_size("head") != 2:
        return lax.all_gather(features, "head", axis=1, tiled=True)
    mine = lax.axis_index("head") * features.shape[1]
    whole = jnp.zeros((features.shape[0], 2 * features.shape[1]), features.dtype)
    whole = lax.dynamic_update_slice(whole, features, (0, mine))
    return lax.dynamic_update_slice(
        whole, from_partner(features, "head"), (0, features.shape[1] - mine)
    )


QUERY_ROWS = 256


def attend_kernel(group_size, low_ref, q_ref, k_ref, v_ref, g_ref, out_ref, dk_ref, dv_ref):
    dk_ref[...] = jnp.zeros_like(dk_ref)
    dv_ref[...] = jnp.zeros_like(dv_ref)
    reach = WINDOW + QUERY_ROWS
    nt = (((1,), (1,)), ((), ()))
    tn = (((0,), (0,)), ((), ()))

    def mul(a, b, dims=(((1,), (0,)), ((), ()))):
        return lax.dot_general(a, b, dims, preferred_element_type=jnp.float32)

    for first in range(0, q_ref.shape[0], QUERY_ROWS):
        rows = slice(first, first + QUERY_ROWS)
        span = slice(first, first + reach)
        keys, values = k_ref[span, :], v_ref[span, :]
        key_at = lax.broadcasted_iota(jnp.int32, (reach, QUERY_ROWS), 0) + (first - WINDOW)
        query_at = lax.broadcasted_iota(jnp.int32, (reach, QUERY_ROWS), 1) + first
        allowed = (key_at >= low_ref[:, rows]) & (key_at <= query_at)
        for head in range(group_size):
            cols = slice(head * HEAD_DIM, (head + 1) * HEAD_DIM)
            query, grad = q_ref[rows, cols], g_ref[rows, cols]
            scores = jnp.where(allowed, mul(keys, query, nt), -jnp.inf)
            weights = jnp.exp(scores - jnp.max(scores, axis=0, keepdims=True))
            probs = weights * (1.0 / jnp.sum(weights, axis=0, keepdims=True))
            probs_low = probs.astype(jnp.bfloat16)
            attended = mul(values, probs_low, tn).astype(jnp.bfloat16).astype(jnp.float32)
            out_ref[rows, cols] = attended.T.astype(jnp.bfloat16)
            out_dot = jnp.sum(attended * grad.astype(jnp.float32).T, axis=0, keepdims=True)
            score_grad = (probs * (mul(values, grad, nt) - out_dot)).astype(jnp.bfloat16)
            dk_ref[span, :] += mul(score_grad, query)
            dv_ref[span, :] += mul(probs_low, grad)


def attend(low, queries, keys, values, grads):
    tok_rows, key_rows = queries.shape[0], keys.shape[0]
    heads = keys.shape[1] // HEAD_DIM
    group_size = queries.shape[1] // keys.shape[1]
    wide = pl.BlockSpec((tok_rows, group_size * HEAD_DIM), lambda h: (0, h))
    tall = pl.BlockSpec((key_rows, HEAD_DIM), lambda h: (0, h))
    sums = jax.ShapeDtypeStruct(keys.shape, jnp.float32)
    work = queries.shape[0] * queries.shape[1] * (WINDOW + QUERY_ROWS)
    return pl.pallas_call(
        functools.partial(attend_kernel, group_size),
        grid=(heads,),
        in_specs=[pl.BlockSpec((1, tok_rows), lambda h: (0, 0)), wide, tall, tall, wide],
        out_specs=[wide, tall, tall],
        out_shape=[jax.ShapeDtypeStruct(queries.shape, jnp.bfloat16), sums, sums],
        compiler_params=pltpu.CompilerParams(vmem_limit_bytes=40 * 1024 * 1024),
        cost_estimate=pl.CostEstimate(
            flops=10 * work, bytes_accessed=8 * queries.size + 12 * keys.size,
            transcendentals=work // HEAD_DIM,
        ),
    )(low, queries, keys, values, grads)


def shards(features, query_weight, key_weight, value_weight, doc_lengths, out_grad):
    tok_rows = features.shape[0]
    query_cols = query_weight.shape[1]
    value_cols = key_weight.shape[1]
    query_heads = query_cols // HEAD_DIM
    value_heads = value_cols // HEAD_DIM
    group_size = query_heads // value_heads
    query_scale = (D / HEADS_Q) ** (-0.5)
    ctx_index = lax.axis_index(CTX)
    core = lax.axis_index("core")

    gathered = gather_features(features)
    chips = lax.axis_size("chip")
    ring = ring_of(chips)
    place = jnp.asarray([ring.index(chip) for chip in range(chips)], jnp.int32)
    here = place[lax.axis_index("chip")]
    owners = jnp.asarray(ring, jnp.int32)[(here + jnp.arange(chips, dtype=jnp.int32)) % chips]
    by_owner = gathered.T.reshape(2 * chips, D // (2 * chips), tok_rows)

    def blocks_of(side):
        return jnp.concatenate(
            [
                lax.dynamic_index_in_dim(by_owner, owners[k] * 2 + side, 0, keepdims=False)
                for k in range(chips)
            ],
            axis=0,
        )

    kept, given = blocks_of(core), blocks_of(1 - core)
    chip_features = jnp.concatenate([kept, from_partner(given, "core")], axis=1)
    deep = D // (2 * chips)

    starts = jnp.cumsum(doc_lengths) - doc_lengths
    query_index = ctx_index * tok_rows + jnp.arange(tok_rows, dtype=jnp.int32)
    query_start = start_of(query_index, starts)
    cosine, sine_table = rope_tables(query_index - query_start)
    local = jnp.arange(tok_rows, dtype=jnp.int32)
    low = jnp.maximum(local - (WINDOW - 1), query_start - ctx_index * tok_rows)[None, :]

    def projected(shards_by_place):
        total = 0.0
        for k, mine in shards_by_place.items():
            rows = slice(k * deep, (k + 1) * deep)
            for block, weights in ((kept, mine), (given, from_partner(mine, "core"))):
                total = total + lax.dot_general(
                    block[rows], weights, (((0,), (0,)), ((), ())),
                    preferred_element_type=jnp.float32,
                )
        return total

    kv_shards = ring_gather(jnp.concatenate([key_weight, value_weight], axis=1))
    query_weight, early = lax.optimization_barrier((query_weight, kv_shards[2]))
    q_shards = ring_gather(query_weight)

    proj = projected(kv_shards)
    own_keys = rotate(proj[:, :value_cols].reshape(tok_rows, -1, HEAD_DIM), cosine, sine_table)
    own = jnp.concatenate([own_keys.reshape(tok_rows, value_cols), proj[:, value_cols:]], axis=1)
    own = own.astype(jnp.bfloat16)
    block = jnp.concatenate([moved(own, far) for far in range(SPAN, 0, -1)] + [own], axis=0)

    proj = projected(q_shards).reshape(tok_rows, query_heads, HEAD_DIM)
    queries = (rotate(proj, cosine, sine_table) * query_scale).astype(jnp.bfloat16)
    attended, key_partial, value_partial = attend(
        low,
        queries.reshape(tok_rows, query_cols),
        block[:, :value_cols],
        block[:, value_cols:],
        out_grad,
    )

    def returned(both):
        total = both[SPAN * tok_rows :]
        for far in range(1, SPAN + 1):
            piece = both[(SPAN - far) * tok_rows : (SPAN - far + 1) * tok_rows]
            total = total + moved(piece.astype(jnp.bfloat16), -far).astype(jnp.float32)
        return total

    key_grad = unrotate(
        returned(key_partial).reshape(tok_rows, value_heads, HEAD_DIM), cosine, sine_table
    ).reshape(tok_rows, value_cols)
    pair_grads = jnp.concatenate([key_grad, returned(value_partial)], axis=1).astype(jnp.bfloat16)
    chip_grads = jnp.concatenate([pair_grads, from_partner(pair_grads, "core")], axis=0)

    def term(k):
        return jnp.dot(
            chip_features[k * deep : (k + 1) * deep], chip_grads,
            preferred_element_type=jnp.float32,
        )

    weight_grads = ring_scatter(term)
    return (
        attended,
        weight_grads[:, :value_cols].astype(jnp.bfloat16),
        weight_grads[:, value_cols:].astype(jnp.bfloat16),
    )


def solution(mesh):
    ctx, head = mesh.shape["ctx"], mesh.shape["head"]
    split = Mesh(mesh.devices.reshape(ctx // 2, 2, head), ("chip", "core", "head"))
    placed = P(CTX, "head")
    return jax.shard_map(
        shards,
        mesh=split,
        in_specs=(placed, placed, placed, placed, P(), placed),
        out_specs=(placed, placed, placed),
        check_vma=False,
    )
```

time: 1040 us -> 692 us (0.67)
  waiting for transfers between devices: 643 us -> 278 us
  Pallas kernels: 0 us -> 52.1 us
  local copies, waits for them, and re-layouts: 71.4 us -> 35 us
  starting transfers between devices: 52 us -> 82.4 us
    all_gather x6 -> x0, waiting for transfers between devices: 362 us -> none  [gathered_rows(): mine = lax.all_gather(piece, 'chip', axis=0, tiled=True)]
    reduce_scatter x4 -> x0, waiting for transfers between devices: 260 us -> none  [shards(): summed = lax.psum_scatter(term, 'chip', scatter_dimension=0, tiled=True)]
    ppermute x0 -> x24, waiting for transfers between devices: none -> 228 us  [along_ring(): return lax.ppermute(block, 'chip', route)]
    pallas_call x0 -> x1, Pallas kernels: none -> 52.1 us  [attend(): pl.pallas_call(functools.partial(attend_kernel, group_size), grid=(heads,...]
    sub x4 -> x0, matrix products: 39.3 us -> none  [attend(): raw_weights = jnp.where(allowed, jnp.exp(scores - row_max), 0.0)]
    ppermute x0 -> x24, starting transfers between devices: none -> 34.4 us  [along_ring(): return lax.ppermute(block, 'chip', route)]
    ppermute x12 -> x6, waiting for transfers between devices: 13.6 us -> 43.9 us  [moved(): return lax.ppermute(block, CTX, route)]
    dot_general x28 -> x40, matrix products: 148 us -> 177 us  [the longest x32 149 us: projected(): lax.dot_general(block[rows], weights, (((0,), (0,)), ((), ())), preferred...]
  transfers between devices with their start and end apart: 34 -> 49, of which waited for: 19 -> 20; matrix products, arithmetic and copies ran while one was open for 29% -> 30% of each run, Pallas kernels for 0% -> 0%
where the time goes in v2:
time: 692 us; the launch traced here: 683 us
  waiting for transfers between devices  278 us (40%)
  matrix products  177 us (26%)
  starting transfers between devices  82.4 us (12%)
  other arithmetic  52.6 us (8%)
  Pallas kernels  52.1 us (8%)
  local copies, waits for them, and re-layouts  35 us (5%)
    ppermute x24, waiting for transfers between devices, along_ring(): return lax.ppermute(block, 'chip', route)  228 us
    dot_general x32, matrix products, projected(): lax.dot_general(block[rows], weights, (((0,), (0,)), ((), ())), preferred...  149 us
    pallas_call x1, Pallas kernels, attend(): pl.pallas_call(functools.partial(attend_kernel, group_size), grid=(heads,...  52.1 us
    ppermute x6, waiting for transfers between devices, moved(): return lax.ppermute(block, CTX, route)  43.9 us
    ppermute x19, starting transfers between devices, from_partner(): return lax.ppermute(block, axis, [(0, 1), (1, 0)])  37.9 us
    ppermute x24, starting transfers between devices, along_ring(): return lax.ppermute(block, 'chip', route)  34.4 us
    dot_general x8, matrix products, term(): jnp.dot(chip_features[k * deep:(k + 1) * deep], chip_grads, preferred_ele...  27.7 us
    concatenate x1, other arithmetic, shards(): jnp.concatenate([moved(own, far) for far in range(SPAN, 0, -1)] + [own],...  19.3 us
  transfers between devices with their start and end apart: 49, of which 20 were waited for; matrix products, arithmetic and copies ran while one was open for 30% of the time, Pallas kernels for 0%

profile of v2, /device:TPU:0, one launch (start us, length us, event | category | flops | bytes accessed | tf_op | source)
XLA Modules:
  0.0 683.1 jit_solution(3142983046246683848)
XLA Ops:
  14.5 23.7 %collective-permute-done.1 = bf16[336,2048]{1,0:T(8,128)(2,1)} collective-permute-done((bf16[336,2048]{1,0:T(8,128)(2,1)}, bf16[336,2048]{1,0:T(8,128)(2,1)}, u32[]{:S(2)}, u32[]{:S(2)}) %collective-permute-start.1) | collective-permute-done | bytes 1376288 | tf_op jit(solution)/shard_map/ppermute | solution.py:38
  51.2 18.6 %collective-permute-done.2 = bf16[336,2048]{1,0:T(8,128)(2,1)} collective-permute-done((bf16[336,2048]{1,0:T(8,128)(2,1)}, bf16[336,2048]{1,0:T(8,128)(2,1)}, u32[]{:S(2)}, u32[]{:S(2)}) %collective-permute-start.2) | collective-permute-done | bytes 1376288 | tf_op jit(solution)/shard_map/ppermute | solution.py:38
  83.7 4.6 fusion.55
  93.3 4.6 fusion.71
  99.8 4.6 fusion.75
  110.9 22.9 %collective-permute-done.28 = bf16[336,2048]{1,0:T(8,128)(2,1)S(1)} collective-permute-done((bf16[336,2048]{1,0:T(8,128)(2,1)}, bf16[336,2048]{1,0:T(8,128)(2,1)S(1)}, u32[]{:S(2)}, u32[]{:S(2)}) %collective-permute-start.28) | collective-permute-done | bytes 1376288 | tf_op jit(solution)/shard_map/ppermute | solution.py:38
  138.4 14.9 %collective-permute-done.4 = bf16[336,2048]{1,0:T(8,128)(2,1)S(1)} collective-permute-done((bf16[336,2048]{1,0:T(8,128)(2,1)S(1)}, bf16[336,2048]{1,0:T(8,128)(2,1)S(1)}, u32[]{:S(2)}, u32[]{:S(2)}) %collective-permute-start.4) | collective-permute-done | bytes 1376288 | tf_op jit(solution)/shard_map/ppermute | solution.py:38
  179.4 7.3 %collective-permute-done.10 = bf16[336,2048]{1,0:T(8,128)(2,1)} collective-permute-done((bf16[336,2048]{1,0:T(8,128)(2,1)S(1)}, bf16[336,2048]{1,0:T(8,128)(2,1)}, u32[]{:S(2)}, u32[]{:S(2)}) %collective-permute-start.10) | collective-permute-done | bytes 1376288 | tf_op jit(solution)/shard_map/ppermute | solution.py:38
  186.7 4.6 fusion.49
  191.3 6.5 collective-permute-done.8
  197.8 4.7 fusion.57
  207.4 8.2 %collective-permute-start.12 = (bf16[336,2048]{1,0:T(8,128)(2,1)}, bf16[336,2048]{1,0:T(8,128)(2,1)}, u32[]{:S(2)}, u32[]{:S(2)}) collective-permute-start(bf16[336,2048]{1,0:T(8,128)(2,1)} %collective-permute-done.8), channel_id=1, source_target_pairs={{0,4},{8,0},{16,8},{24,16},{28,24},{20,28},{12,20},{4,12},{1,5},{9... | collective-permute-start | bytes 4128776 | tf_op jit(solution)/shard_map/ppermute | solution.py:38
  226.1 20.6 %add_add_fusion = f32[512,2048]{1,0:T(8,128)} fusion(f32[512,2048]{1,0:T(8,128)} %fusion.21, f32[512,2048]{1,0:T(8,128)} %fusion.25, f32[512,2048]{1,0:T(8,128)} %fusion.31, f32[512,2048]{1,0:T(8,128)} %fusion.35, f32[512,2048]{1,0:T(8,128)} %fusion.39, f32[512,2048]{1,0:T(8,128)} %fusion.43, f32[512,2048]{1,0:T(8,128)S(1)} %fusion.47, ...), kind=kOutput, calls=%fused_computation.23 | convolution fusion | flops 720371712 | bytes 68829184 | tf_op jit(solution)/shard_map/dot_general | solution.py:210
  258.2 4.6 fusion.41
  274.3 4.6 fusion.45
  283.5 5.9 collective-permute-done.16
  289.5 29.4 %collective-permute-done.17 = bf16[336,1024]{1,0:T(8,128)(2,1)S(1)} collective-permute-done((bf16[336,1024]{1,0:T(8,128)(2,1)S(1)}, bf16[336,1024]{1,0:T(8,128)(2,1)S(1)}, u32[]{:S(2)}, u32[]{:S(2)}) %collective-permute-start.17) | collective-permute-done | bytes 688160 | tf_op jit(solution)/shard_map/ppermute | solution.py:38
  318.9 20.1 %collective-permute-start.18 = (bf16[336,2048]{1,0:T(8,128)(2,1)S(1)}, bf16[336,2048]{1,0:T(8,128)(2,1)S(1)}, u32[]{:S(2)}, u32[]{:S(2)}) collective-permute-start(bf16[336,2048]{1,0:T(8,128)(2,1)S(1)} %constant_dynamic-update-slice_fusion.2), channel_id=1, source_target_pairs={{0,2},{2,0},{1,3},{3,1},{4,6},{6,4},{5,7},{7,5},{8,10},{10,8},{9,1... | collective-permute-start | bytes 4128776 | tf_op jit(solution)/shard_map/ppermute | solution.py:28
  345.5 19.3 %maximum_maximum_fusion = bf16[1536,2048]{1,0:T(8,128)(2,1)} fusion(bf16[512,1024]{1,0:T(8,128)(2,1)S(1)} %slice.281, bf16[512,1024]{1,0:T(8,128)(2,1)S(1)} %fusion.3, bf16[512,2048]{1,0:T(8,128)(2,1)S(1)} %collective-permute-done.34, bf16[512,2048]{1,0:T(8,128)(2,1)S(1)} %collective-permute-done.33), kind=kLoop, calls=%fused_computation.15 | loop fusion | flops 25165824 | bytes 12582912 | tf_op jit(solution)/shard_map/concatenate | solution.py:224
  371.7 19.9 %add_add_fusion.1 = f32[512,2048]{1,0:T(8,128)S(1)} fusion(f32[512,2048]{1,0:T(8,128)} %fusion.23, f32[512,2048]{1,0:T(8,128)} %fusion.27, f32[512,2048]{1,0:T(8,128)} %fusion.33, f32[512,2048]{1,0:T(8,128)} %fusion.37, f32[512,2048]{1,0:T(8,128)} %fusion.41, f32[512,2048]{1,0:T(8,128)} %fusion.45, f32[512,2048]{1,0:T(8,128)} %fusion.49, ...), kind=kOutput, calls=%fused_computation.24 | convolution fusion | flops 720371712 | bytes 68829184 | tf_op jit(solution)/shard_map/dot_general | solution.py:210
  392.5 4.7 slice_negate_fusion
  397.2 6.7 maximum_multiply_fusion
  406.2 8.3 %fusion.1.q_ref = bf16[512,2048]{1,0:T(8,128)(2,1)S(1)} fusion(f32[64,8,16,128]{3,2,1,0:T(8,128)} %bitcast.239, f32[512,2048]{1,0:T(8,128)S(1)} %add_add_fusion.1, f32[64,8,16,128]{3,2,1,0:T(8,128)} %bitcast.240), kind=kLoop, calls=%fused_computation.18 | loop fusion | flops 4194304 | bytes 14680064 | tf_op jit(solution)/shard_map/convert_element_type | solution.py:227
  414.5 52.1 %shard_map.103 = (bf16[512,2048]{1,0:T(8,128)(2,1)}, f32[1536,1024]{1,0:T(8,128)}, f32[1536,1024]{1,0:T(8,128)}) custom-call(s32[1,512]{1,0:T(1,128)S(1)} %add_maximum_fusion.low_ref, bf16[512,2048]{1,0:T(8,128)(2,1)S(1)} %fusion.1.q_ref, bf16[1536,1024]{1,0:T(8,128)(2,1)S(1)} %get-tuple-element.12.k_ref, bf16[1536,1024]{1,0:T(8,128)(2,1)S(1)} %get-tuple-element.11.v_ref, ...), custom_call_target="tpu_custom_call" | custom-call | flops 13421772800 | bytes 27262976 | tf_op jit(solution)/shard_map/pallas_call | solution.py:152
  483.1 15.6 %collective-permute-done.37 = bf16[512,1024]{1,0:T(8,128)(2,1)S(1)} collective-permute-done((bf16[512,1024]{1,0:T(8,128)(2,1)S(1)}, bf16[512,1024]{1,0:T(8,128)(2,1)S(1)}, u32[]{:S(2)}, u32[]{:S(2)}) %collective-permute-start.37) | collective-permute-done | bytes 1048608 | tf_op jit(solution)/shard_map/ppermute | solution.py:24
  503.5 28.3 %collective-permute-done.39 = bf16[512,1024]{1,0:T(8,128)(2,1)S(1)} collective-permute-done((bf16[512,1024]{1,0:T(8,128)(2,1)S(1)}, bf16[512,1024]{1,0:T(8,128)(2,1)S(1)}, u32[]{:S(2)}, u32[]{:S(2)}) %collective-permute-start.39) | collective-permute-done | bytes 1048608 | tf_op jit(solution)/shard_map/ppermute | solution.py:24
  532.6 11.1 %collective-permute-start.40 = (bf16[512,2048]{1,0:T(8,128)(2,1)S(1)}, bf16[512,2048]{1,0:T(8,128)(2,1)S(1)}, u32[]{:S(2)}, u32[]{:S(2)}) collective-permute-start(bf16[512,2048]{1,0:T(8,128)(2,1)S(1)} %pad_maximum_fusion.2), channel_id=1, source_target_pairs={{0,2},{2,0},{1,3},{3,1},{4,6},{6,4},{5,7},{7,5},{8,10},{10,8},{9,1... | collective-permute-start | bytes 6291464 | tf_op jit(solution)/shard_map/ppermute | solution.py:28
  552.9 15.5 %collective-permute-done.45 = bf16[336,1024]{1,0:T(8,128)(2,1)S(1)} collective-permute-done((bf16[336,1024]{1,0:T(8,128)(2,1)S(1)}, bf16[336,1024]{1,0:T(8,128)(2,1)S(1)}, u32[]{:S(2)}, u32[]{:S(2)}) %collective-permute-start.45) | collective-permute-done | bytes 688160 | tf_op jit(solution)/shard_map/ppermute | solution.py:38
  568.4 9.6 %add_convert_fusion.3 = bf16[336,2048]{1,0:T(8,128)(2,1)S(1)} fusion(bf16[336,1024]{1,0:T(8,128)(2,1)S(1)} %collective-permute-done.45, bf16[2688,512]{1,0:T(8,128)(2,1)} %collective-permute-done.35, bf16[2688,512]{1,0:T(8,128)(2,1)S(1)} %bitcast_dynamic-update-slice_fusion.11, bf16[512,2048]{1,0:T(8,128)(2,1)S(1)} %collective-permute-done.40, ...), kind=kOutput, calls=%fused_computation.28 | convolution fusion | flops 1425309696 | bytes 11763712 | tf_op jit(solution)/shard_map/dot_general | solution.py:250
  583.1 26.8 %collective-permute-done.46 = bf16[336,2048]{1,0:T(8,128)(2,1)S(1)} collective-permute-done((bf16[336,2048]{1,0:T(8,128)(2,1)S(1)}, bf16[336,2048]{1,0:T(8,128)(2,1)S(1)}, u32[]{:S(2)}, u32[]{:S(2)}) %collective-permute-start.46) | collective-permute-done | bytes 1376288 | tf_op jit(solution)/shard_map/ppermute | solution.py:38
  617.9 26.9 %collective-permute-done.47 = bf16[336,2048]{1,0:T(8,128)(2,1)S(1)} collective-permute-done((bf16[336,2048]{1,0:T(8,128)(2,1)S(1)}, bf16[336,2048]{1,0:T(8,128)(2,1)S(1)}, u32[]{:S(2)}, u32[]{:S(2)}) %collective-permute-start.47) | collective-permute-done | bytes 1376288 | tf_op jit(solution)/shard_map/ppermute | solution.py:38
  654.7 23.4 %collective-permute-done.48 = bf16[336,2048]{1,0:T(8,128)(2,1)S(1)} collective-permute-done((bf16[336,2048]{1,0:T(8,128)(2,1)S(1)}, bf16[336,2048]{1,0:T(8,128)(2,1)S(1)}, u32[]{:S(2)}, u32[]{:S(2)}) %collective-permute-start.48) | collective-permute-done | bytes 1376288 | tf_op jit(solution)/shard_map/ppermute | solution.py:38
  (207 shorter events, 197.4 us)
Async XLA Ops:
  4.6 33.5 %collective-permute-start.1 = (bf16[336,2048]{1,0:T(8,128)(2,1)}, bf16[336,2048]{1,0:T(8,128)(2,1)}, u32[]{:S(2)}, u32[]{:S(2)}) collective-permute-start(bf16[336,2048]{1,0:T(8,128)(2,1)} %constant_dynamic-update-slice_fusion), channel_id=1, source_target_pairs={{0,4},{8,0},{16,8},{24,16},{28,24},{20,28},{12,20},{4,12},{1,5},{9... | collective-permute-start | bytes 4128776 | tf_op jit(solution)/shard_map/ppermute | solution.py:38
  10.9 61.3 %collective-permute-start = (bf16[512,2688]{0,1:T(8,128)(2,1)S(1)}, bf16[512,2688]{0,1:T(8,128)(2,1)}, u32[]{:S(2)}, u32[]{:S(2)}) collective-permute-start(bf16[512,2688]{0,1:T(8,128)(2,1)S(1)} %copy.13), channel_id=1, source_target_pairs={{0,1},{1,0},{2,3},{3,2},{4,5},{5,4},{6,7},{7,6},{8,9},{9,8},{10,11... | collective-permute-start | bytes 8257544 | tf_op jit(solution)/shard_map/ppermute | solution.py:28
  12.9 80.0 %collective-permute-start.19 = (bf16[336,2048]{1,0:T(8,128)(2,1)}, bf16[336,2048]{1,0:T(8,128)(2,1)}, u32[]{:S(2)}, u32[]{:S(2)}) collective-permute-start(bf16[336,2048]{1,0:T(8,128)(2,1)} %constant_dynamic-update-slice_fusion), channel_id=1, source_target_pairs={{0,2},{2,0},{1,3},{3,1},{4,6},{6,4},{5,7},{7,5},{8,10},{10,8},{9,1... | collective-permute-start | bytes 4128776 | tf_op jit(solution)/shard_map/ppermute | solution.py:28
  44.1 32.6 %collective-permute-start.24 = (bf16[336,2048]{1,0:T(8,128)(2,1)}, bf16[336,2048]{1,0:T(8,128)(2,1)}, u32[]{:S(2)}, u32[]{:S(2)}) collective-permute-start(bf16[336,2048]{1,0:T(8,128)(2,1)} %collective-permute-done.21), channel_id=1, source_target_pairs={{0,8},{8,16},{16,24},{24,28},{28,20},{20,12},{12,4},{4,0},{1,9},{9... | collective-permute-start | bytes 4128776 | tf_op jit(solution)/shard_map/ppermute | solution.py:38
  51.1 46.8 %collective-permute-start.22 = (bf16[336,2048]{1,0:T(8,128)(2,1)}, bf16[336,2048]{1,0:T(8,128)(2,1)S(1)}, u32[]{:S(2)}, u32[]{:S(2)}) collective-permute-start(bf16[336,2048]{1,0:T(8,128)(2,1)} %collective-permute-done.21), channel_id=1, source_target_pairs={{0,2},{2,0},{1,3},{3,1},{4,6},{6,4},{5,7},{7,5},{8,10},{10,8},{9,1... | collective-permute-start | bytes 4128776 | tf_op jit(solution)/shard_map/ppermute | solution.py:28
  69.8 34.6 %collective-permute-start.20 = (bf16[336,2048]{1,0:T(8,128)(2,1)}, bf16[336,2048]{1,0:T(8,128)(2,1)S(1)}, u32[]{:S(2)}, u32[]{:S(2)}) collective-permute-start(bf16[336,2048]{1,0:T(8,128)(2,1)} %collective-permute-done.1), channel_id=1, source_target_pairs={{0,2},{2,0},{1,3},{3,1},{4,6},{6,4},{5,7},{7,5},{8,10},{10,8},{9,1... | collective-permute-start | bytes 4128776 | tf_op jit(solution)/shard_map/ppermute | solution.py:28
  72.2 62.3 %collective-permute-start.6 = (bf16[336,2048]{1,0:T(8,128)(2,1)S(1)}, bf16[336,2048]{1,0:T(8,128)(2,1)S(1)}, u32[]{:S(2)}, u32[]{:S(2)}) collective-permute-start(bf16[336,2048]{1,0:T(8,128)(2,1)S(1)} %copy-done.5), channel_id=1, source_target_pairs={{0,8},{8,16},{16,24},{24,28},{28,20},{20,12},{12,4},{4,0},{1,9},{9... | collective-permute-start | bytes 4128776 | tf_op jit(solution)/shard_map/ppermute | solution.py:38
  76.7 57.0 %collective-permute-start.28 = (bf16[336,2048]{1,0:T(8,128)(2,1)}, bf16[336,2048]{1,0:T(8,128)(2,1)S(1)}, u32[]{:S(2)}, u32[]{:S(2)}) collective-permute-start(bf16[336,2048]{1,0:T(8,128)(2,1)} %collective-permute-done.24), channel_id=1, source_target_pairs={{0,8},{8,16},{16,24},{24,28},{28,20},{20,12},{12,4},{4,0},{1,9},{9... | collective-permute-start | bytes 4128776 | tf_op jit(solution)/shard_map/ppermute | solution.py:38
  92.9 40.9 %collective-permute-start.26 = (bf16[336,2048]{1,0:T(8,128)(2,1)}, bf16[336,2048]{1,0:T(8,128)(2,1)S(1)}, u32[]{:S(2)}, u32[]{:S(2)}) collective-permute-start(bf16[336,2048]{1,0:T(8,128)(2,1)} %collective-permute-done.2), channel_id=1, source_target_pairs={{0,4},{8,0},{16,8},{24,16},{28,24},{20,28},{12,20},{4,12},{1,5},{9... | collective-permute-start | bytes 4128776 | tf_op jit(solution)/shard_map/ppermute | solution.py:38
  97.9 55.3 %collective-permute-start.4 = (bf16[336,2048]{1,0:T(8,128)(2,1)S(1)}, bf16[336,2048]{1,0:T(8,128)(2,1)S(1)}, u32[]{:S(2)}, u32[]{:S(2)}) collective-permute-start(bf16[336,2048]{1,0:T(8,128)(2,1)S(1)} %copy-done.5), channel_id=1, source_target_pairs={{0,4},{8,0},{16,8},{24,16},{28,24},{20,28},{12,20},{4,12},{1,5},{9... | collective-permute-start | bytes 4128776 | tf_op jit(solution)/shard_map/ppermute | solution.py:38
  104.4 52.6 %collective-permute-start.3 = (bf16[336,2048]{1,0:T(8,128)(2,1)S(1)}, bf16[336,2048]{1,0:T(8,128)(2,1)S(1)}, u32[]{:S(2)}, u32[]{:S(2)}) collective-permute-start(bf16[336,2048]{1,0:T(8,128)(2,1)S(1)} %copy-done.5), channel_id=1, source_target_pairs={{0,2},{2,0},{1,3},{3,1},{4,6},{6,4},{5,7},{7,5},{8,10},{10,8},{9,1... | collective-permute-start | bytes 4128776 | tf_op jit(solution)/shard_map/ppermute | solution.py:28
  133.7 34.7 %collective-permute-start.25 = (bf16[336,2048]{1,0:T(8,128)(2,1)}, bf16[336,2048]{1,0:T(8,128)(2,1)S(1)}, u32[]{:S(2)}, u32[]{:S(2)}) collective-permute-start(bf16[336,2048]{1,0:T(8,128)(2,1)} %collective-permute-done.24), channel_id=1, source_target_pairs={{0,2},{2,0},{1,3},{3,1},{4,6},{6,4},{5,7},{7,5},{8,10},{10,8},{9,1... | collective-permute-start | bytes 4128776 | tf_op jit(solution)/shard_map/ppermute | solution.py:28
  133.8 38.3 %collective-permute-start.23 = (bf16[336,2048]{1,0:T(8,128)(2,1)}, bf16[336,2048]{1,0:T(8,128)(2,1)S(1)}, u32[]{:S(2)}, u32[]{:S(2)}) collective-permute-start(bf16[336,2048]{1,0:T(8,128)(2,1)} %collective-permute-done.2), channel_id=1, source_target_pairs={{0,2},{2,0},{1,3},{3,1},{4,6},{6,4},{5,7},{7,5},{8,10},{10,8},{9,1... | collective-permute-start | bytes 4128776 | tf_op jit(solution)/shard_map/ppermute | solution.py:28
  134.5 40.9 %collective-permute-start.30 = (bf16[336,1024]{1,0:T(8,128)(2,1)S(1)}, bf16[336,1024]{1,0:T(8,128)(2,1)S(1)}, u32[]{:S(2)}, u32[]{:S(2)}) collective-permute-start(bf16[336,1024]{1,0:T(8,128)(2,1)S(1)} %slice.181), channel_id=1, source_target_pairs={{0,8},{8,16},{16,24},{24,28},{28,20},{20,12},{12,4},{4,0},{1,9},{9... | collective-permute-start | bytes 2064392 | tf_op jit(solution)/shard_map/ppermute | solution.py:38
  175.4 32.0 %collective-permute-start.5 = (bf16[336,2048]{1,0:T(8,128)(2,1)S(1)}, bf16[336,2048]{1,0:T(8,128)(2,1)S(1)}, u32[]{:S(2)}, u32[]{:S(2)}) collective-permute-start(bf16[336,2048]{1,0:T(8,128)(2,1)S(1)} %collective-permute-done.4), channel_id=1, source_target_pairs={{0,2},{2,0},{1,3},{3,1},{4,6},{6,4},{5,7},{7,5},{8,10},{10,8},{9,1... | collective-permute-start | bytes 4128776 | tf_op jit(solution)/shard_map/ppermute | solution.py:28
  176.0 42.9 %collective-permute-start.27 = (bf16[336,2048]{1,0:T(8,128)(2,1)S(1)}, bf16[336,2048]{1,0:T(8,128)(2,1)S(1)}, u32[]{:S(2)}, u32[]{:S(2)}) collective-permute-start(bf16[336,2048]{1,0:T(8,128)(2,1)S(1)} %collective-permute-done.26), channel_id=1, source_target_pairs={{0,2},{2,0},{1,3},{3,1},{4,6},{6,4},{5,7},{7,5},{8,10},{10,8},{9,1... | collective-permute-start | bytes 4128776 | tf_op jit(solution)/shard_map/ppermute | solution.py:28
  186.7 39.4 %collective-permute-start.29 = (bf16[336,2048]{1,0:T(8,128)(2,1)S(1)}, bf16[336,2048]{1,0:T(8,128)(2,1)}, u32[]{:S(2)}, u32[]{:S(2)}) collective-permute-start(bf16[336,2048]{1,0:T(8,128)(2,1)S(1)} %collective-permute-done.28), channel_id=1, source_target_pairs={{0,2},{2,0},{1,3},{3,1},{4,6},{6,4},{5,7},{7,5},{8,10},{10,8},{9,1... | collective-permute-start | bytes 4128776 | tf_op jit(solution)/shard_map/ppermute | solution.py:28
  202.5 60.3 %collective-permute-start.14 = (bf16[336,2048]{1,0:T(8,128)(2,1)}, bf16[336,2048]{1,0:T(8,128)(2,1)}, u32[]{:S(2)}, u32[]{:S(2)}) collective-permute-start(bf16[336,2048]{1,0:T(8,128)(2,1)} %collective-permute-done.10), channel_id=1, source_target_pairs={{0,8},{8,16},{16,24},{24,28},{28,20},{20,12},{12,4},{4,0},{1,9},{9... | collective-permute-start | bytes 4128776 | tf_op jit(solution)/shard_map/ppermute | solution.py:38
  207.4 48.3 %collective-permute-start.12 = (bf16[336,2048]{1,0:T(8,128)(2,1)}, bf16[336,2048]{1,0:T(8,128)(2,1)}, u32[]{:S(2)}, u32[]{:S(2)}) collective-permute-start(bf16[336,2048]{1,0:T(8,128)(2,1)} %collective-permute-done.8), channel_id=1, source_target_pairs={{0,4},{8,0},{16,8},{24,16},{28,24},{20,28},{12,20},{4,12},{1,5},{9... | collective-permute-start | bytes 4128776 | tf_op jit(solution)/shard_map/ppermute | solution.py:38
  218.9 53.1 %collective-permute-start.11 = (bf16[336,2048]{1,0:T(8,128)(2,1)}, bf16[336,2048]{1,0:T(8,128)(2,1)}, u32[]{:S(2)}, u32[]{:S(2)}) collective-permute-start(bf16[336,2048]{1,0:T(8,128)(2,1)} %collective-permute-done.10), channel_id=1, source_target_pairs={{0,2},{2,0},{1,3},{3,1},{4,6},{6,4},{5,7},{7,5},{8,10},{10,8},{9,1... | collective-permute-start | bytes 4128776 | tf_op jit(solution)/shard_map/ppermute | solution.py:28
  222.3 51.1 %collective-permute-start.9 = (bf16[336,2048]{1,0:T(8,128)(2,1)}, bf16[336,2048]{1,0:T(8,128)(2,1)}, u32[]{:S(2)}, u32[]{:S(2)}) collective-permute-start(bf16[336,2048]{1,0:T(8,128)(2,1)} %collective-permute-done.8), channel_id=1, source_target_pairs={{0,2},{2,0},{1,3},{3,1},{4,6},{6,4},{5,7},{7,5},{8,10},{10,8},{9,1... | collective-permute-start | bytes 4128776 | tf_op jit(solution)/shard_map/ppermute | solution.py:28
  253.6 91.9 %collective-permute-start.34 = (bf16[512,2048]{1,0:T(8,128)(2,1)S(1)}, bf16[512,2048]{1,0:T(8,128)(2,1)S(1)}, u32[]{:S(2)}, u32[]{:S(2)}) collective-permute-start(bf16[512,2048]{1,0:T(8,128)(2,1)S(1)} %pad_maximum_fusion.1), channel_id=1, source_target_pairs={{0,2},{2,4},{4,6},{6,8},{8,10},{10,12},{12,14},{14,16},{16,18},{18... | collective-permute-start | bytes 6291464 | tf_op jit(solution)/shard_map/ppermute | solution.py:24
  255.7 89.8 %collective-permute-start.33 = (bf16[512,2048]{1,0:T(8,128)(2,1)S(1)}, bf16[512,2048]{1,0:T(8,128)(2,1)S(1)}, u32[]{:S(2)}, u32[]{:S(2)}) collective-permute-start(bf16[512,2048]{1,0:T(8,128)(2,1)S(1)} %pad_maximum_fusion.1), channel_id=1, source_target_pairs={{0,4},{2,6},{4,8},{6,10},{8,12},{10,14},{12,16},{14,18},{16,20},{1... | collective-permute-start | bytes 6291464 | tf_op jit(solution)/shard_map/ppermute | solution.py:24
  262.8 79.4 %collective-permute-start.13 = (bf16[336,2048]{1,0:T(8,128)(2,1)}, bf16[336,2048]{1,0:T(8,128)(2,1)S(1)}, u32[]{:S(2)}, u32[]{:S(2)}) collective-permute-start(bf16[336,2048]{1,0:T(8,128)(2,1)} %collective-permute-done.12), channel_id=1, source_target_pairs={{0,2},{2,0},{1,3},{3,1},{4,6},{6,4},{5,7},{7,5},{8,10},{10,8},{9,1... | collective-permute-start | bytes 4128776 | tf_op jit(solution)/shard_map/ppermute | solution.py:28
  273.4 45.5 %collective-permute-start.17 = (bf16[336,1024]{1,0:T(8,128)(2,1)S(1)}, bf16[336,1024]{1,0:T(8,128)(2,1)S(1)}, u32[]{:S(2)}, u32[]{:S(2)}) collective-permute-start(bf16[336,1024]{1,0:T(8,128)(2,1)S(1)} %slice.178), channel_id=1, source_target_pairs={{0,4},{8,0},{16,8},{24,16},{28,24},{20,28},{12,20},{4,12},{1,5},{9... | collective-permute-start | bytes 2064392 | tf_op jit(solution)/shard_map/ppermute | solution.py:38
  289.4 82.3 %collective-permute-start.15 = (bf16[336,2048]{1,0:T(8,128)(2,1)}, bf16[336,2048]{1,0:T(8,128)(2,1)}, u32[]{:S(2)}, u32[]{:S(2)}) collective-permute-start(bf16[336,2048]{1,0:T(8,128)(2,1)} %collective-permute-done.14), channel_id=1, source_target_pairs={{0,2},{2,0},{1,3},{3,1},{4,6},{6,4},{5,7},{7,5},{8,10},{10,8},{9,1... | collective-permute-start | bytes 4128776 | tf_op jit(solution)/shard_map/ppermute | solution.py:28
  318.9 49.5 %collective-permute-start.18 = (bf16[336,2048]{1,0:T(8,128)(2,1)S(1)}, bf16[336,2048]{1,0:T(8,128)(2,1)S(1)}, u32[]{:S(2)}, u32[]{:S(2)}) collective-permute-start(bf16[336,2048]{1,0:T(8,128)(2,1)S(1)} %constant_dynamic-update-slice_fusion.2), channel_id=1, source_target_pairs={{0,2},{2,0},{1,3},{3,1},{4,6},{6,4},{5,7},{7,5},{8,10},{10,8},{9,1... | collective-permute-start | bytes 4128776 | tf_op jit(solution)/shard_map/ppermute | solution.py:28
  478.5 65.5 %collective-permute-start.35 = (bf16[2688,512]{1,0:T(8,128)(2,1)}, bf16[2688,512]{1,0:T(8,128)(2,1)}, u32[]{:S(2)}, u32[]{:S(2)}) collective-permute-start(bf16[2688,512]{1,0:T(8,128)(2,1)} %get-tuple-element.13), channel_id=1, source_target_pairs={{0,2},{2,0},{1,3},{3,1},{4,6},{6,4},{5,7},{7,5},{8,10},{10,8},{9,1... | collective-permute-start | bytes 8257544 | tf_op jit(solution)/shard_map/ppermute | solution.py:28
  480.3 51.5 %collective-permute-start.39 = (bf16[512,1024]{1,0:T(8,128)(2,1)S(1)}, bf16[512,1024]{1,0:T(8,128)(2,1)S(1)}, u32[]{:S(2)}, u32[]{:S(2)}) collective-permute-start(bf16[512,1024]{1,0:T(8,128)(2,1)S(1)} %get-tuple-element.20), channel_id=1, source_target_pairs={{4,0},{6,2},{8,4},{10,6},{12,8},{14,10},{16,12},{18,14},{20,16},{2... | collective-permute-start | bytes 3145736 | tf_op jit(solution)/shard_map/ppermute | solution.py:24
  481.6 50.2 %collective-permute-start.38 = (bf16[512,1024]{1,0:T(8,128)(2,1)S(1)}, bf16[512,1024]{1,0:T(8,128)(2,1)S(1)}, u32[]{:S(2)}, u32[]{:S(2)}) collective-permute-start(bf16[512,1024]{1,0:T(8,128)(2,1)S(1)} %get-tuple-element.19), channel_id=1, source_target_pairs={{2,0},{4,2},{6,4},{8,6},{10,8},{12,10},{14,12},{16,14},{18,16},{20... | collective-permute-start | bytes 3145736 | tf_op jit(solution)/shard_map/ppermute | solution.py:24
  582.8 32.1 %collective-permute-start.42 = (bf16[336,2048]{1,0:T(8,128)(2,1)S(1)}, bf16[336,2048]{1,0:T(8,128)(2,1)S(1)}, u32[]{:S(2)}, u32[]{:S(2)}) collective-permute-start(bf16[336,2048]{1,0:T(8,128)(2,1)S(1)} %add_convert_fusion.6), channel_id=1, source_target_pairs={{0,8},{8,16},{16,24},{24,28},{28,20},{20,12},{12,4},{4,0},{1,9},{9... | collective-permute-start | bytes 4128776 | tf_op jit(solution)/shard_map/ppermute | solution.py:38
  612.5 32.2 %collective-permute-start.47 = (bf16[336,2048]{1,0:T(8,128)(2,1)S(1)}, bf16[336,2048]{1,0:T(8,128)(2,1)S(1)}, u32[]{:S(2)}, u32[]{:S(2)}) collective-permute-start(bf16[336,2048]{1,0:T(8,128)(2,1)S(1)} %add_convert_fusion.2), channel_id=1, source_target_pairs={{0,4},{8,0},{16,8},{24,16},{28,24},{20,28},{12,20},{4,12},{1,5},{9... | collective-permute-start | bytes 4128776 | tf_op jit(solution)/shard_map/ppermute | solution.py:38
  (30 other events, 618.9 us)
